TPU v7x, 128 devices: a whole 4x4x4 slice. The times are simulated.
128 devices in a mesh: attn: 8 (over z, x_lo), ffn: 16 (over y, x_hi, core).
Axes of the slice: x: 4 (x_hi: 2, x_lo: 2; x = x_hi * 2 + x_lo), y: 4, z: 4, core: 2. Of those that a mesh axis runs over, the one named last changes fastest.
Arguments:
- queries: bfloat16 [512, 8192], P(('attn', 'ffn')), may hold values from -400 to 400
- slot_key_cache: bfloat16 [512, 256, 512], P(('attn', 'ffn')), may hold values from -6 to 6
- slot_value_cache: bfloat16 [512, 256, 512], P(('attn', 'ffn')), may hold values from -16 to 16
- fresh_token_key: bfloat16 [512, 512], P(('attn', 'ffn')), may hold values from -6 to 6
- fresh_token_value: bfloat16 [512, 512], P(('attn', 'ffn')), may hold values from -16 to 16
- lengths: int32 [512], P(('attn', 'ffn')), may hold values from 1 to 256, as said below
- slot_of: int32 [512], replicated, may hold values from 0 to 511, each once
- residual: bfloat16 [512, 16384], P(None, 'attn'), may hold values from -4 to 4
- w_out: bfloat16 [8192, 16384], P('ffn', 'attn'), may hold values from -0.0625 to 0.0625
- norm_gain: bfloat16 [16384], P('attn'), may hold values from 0.099609375 to 1.8984375
- w_gate: bfloat16 [16384, 26624], P('attn', 'ffn'), may hold values from -0.046875 to 0.046875
- w_up: bfloat16 [16384, 26624], P('attn', 'ffn'), may hold values from -0.046875 to 0.046875
- w_down: bfloat16 [26624, 16384], P('ffn', 'attn'), may hold values from -0.0390625 to 0.0390625
Outputs:
- layer_out: bfloat16 [512, 16384], P('ffn', 'attn')
Inputs may be any that keep to these rules, and one draw needn't show every extreme that they name: `lengths`: some slot has exactly 256 live positions. `slot_of`: each slot holds exactly one request.
All inputs are finite; a program needn't handle non-finite values.
Results may differ from a plain program's by a relative error of at most 0.011.
Values may be sent and summed in bfloat16 or wider, within the bound.
No kernel may reach another device: no remote copies, remote signals or barrier semaphores. Data moves between devices by JAX's collectives and lax.ppermute only.
A program may use at most 128 MiB of HBM per device.

v0:
```python
import jax
import jax.numpy as jnp
from jax import lax
from jax.sharding import PartitionSpec as P

D = 16384
QUERY_HEADS = 64
KEY_VALUE_HEADS = 4
HEAD_SIZE = 128
SLOT_CAPACITY = 256


epsilon = 1e-05


def attend(queries, slot_key_cache, slot_value_cache, fresh_token_key, fresh_token_value, lengths):
    request_slot_count = queries.shape[0]
    query_group_width = QUERY_HEADS // KEY_VALUE_HEADS
    query_head_rows = queries.reshape(
        request_slot_count, KEY_VALUE_HEADS, query_group_width, HEAD_SIZE
    )
    stored_keys = slot_key_cache.reshape(
        request_slot_count, SLOT_CAPACITY, KEY_VALUE_HEADS, HEAD_SIZE
    )
    stored_values = slot_value_cache.reshape(
        request_slot_count, SLOT_CAPACITY, KEY_VALUE_HEADS, HEAD_SIZE
    )
    current_key = fresh_token_key.reshape(request_slot_count, KEY_VALUE_HEADS, HEAD_SIZE)
    current_value = fresh_token_value.astype(jnp.float32).reshape(
        request_slot_count, KEY_VALUE_HEADS, HEAD_SIZE
    )
    factor = HEAD_SIZE ** (-0.5)
    scores = (
        jnp.einsum(
            "sgqd,spgd->sgqp", query_head_rows, stored_keys, preferred_element_type=jnp.float32
        )
        * factor
    )
    own_score = (
        jnp.einsum(
            "sgqd,sgd->sgq", query_head_rows, current_key, preferred_element_type=jnp.float32
        )
        * factor
    )
    live_mask = jnp.arange(SLOT_CAPACITY, dtype=jnp.int32)[None, :] < lengths[:, None]
    scores = jnp.where(live_mask[:, None, None, :], scores, -jnp.inf)
    highest = jnp.maximum(jnp.max(scores, axis=-1), own_score)
    weights = jnp.exp(scores - highest[..., None])
    own_weight = jnp.exp(own_score - highest)
    weight_sum = jnp.sum(weights, axis=-1) + own_weight
    own_low = own_weight.astype(jnp.bfloat16).astype(jnp.float32)
    combined = jnp.einsum(
        "sgqp,spgd->sgqd",
        weights.astype(jnp.bfloat16),
        stored_values,
        preferred_element_type=jnp.float32,
    )
    combined = combined + own_low[..., None] * current_value[:, :, None, :]
    return (
        (combined / weight_sum[..., None])
        .reshape(request_slot_count, QUERY_HEADS * HEAD_SIZE)
        .astype(jnp.bfloat16)
    )


def normalize(row_state, gain_vector):
    squares = lax.psum(jnp.sum(row_state * row_state, axis=-1), "attn")
    return (row_state * lax.rsqrt(squares / D + epsilon)[:, None] * gain_vector).astype(
        jnp.bfloat16
    )


def local(
    queries,
    slot_key_cache,
    slot_value_cache,
    fresh_token_key,
    fresh_token_value,
    lengths,
    slot_of,
    residual,
    w_out,
    norm_gain,
    w_gate,
    w_up,
    w_down,
):
    attended = attend(
        queries, slot_key_cache, slot_value_cache, fresh_token_key, fresh_token_value, lengths
    )
    exchanged = lax.all_to_all(attended, "ffn", split_axis=1, concat_axis=0, tiled=True)
    partial_value = jnp.dot(
        lax.all_gather(exchanged, "attn", axis=0, tiled=True),
        w_out,
        preferred_element_type=jnp.float32,
    )
    partial_value = jnp.take(partial_value, slot_of, axis=0)
    row_total = residual.shape[0]
    row_share = row_total // lax.axis_size("ffn")
    first_row = lax.axis_index("ffn") * row_share
    gain_vector = norm_gain.astype(jnp.float32)
    summed = lax.psum(partial_value, "ffn")
    hidden_state = residual.astype(jnp.float32) + summed
    normed = normalize(hidden_state, gain_vector)
    kept_state = lax.dynamic_slice_in_dim(hidden_state, first_row, row_share, 0)
    gate_part = jnp.dot(normed, w_gate, preferred_element_type=jnp.float32)
    up_part = jnp.dot(normed, w_up, preferred_element_type=jnp.float32)
    gate_sum, up_sum = lax.psum((gate_part, up_part), "attn")
    hidden = (jax.nn.silu(gate_sum) * up_sum).astype(jnp.bfloat16)
    down_out = lax.psum_scatter(
        jnp.dot(hidden, w_down, preferred_element_type=jnp.float32),
        "ffn",
        scatter_dimension=0,
        tiled=True,
    )
    return (kept_state + down_out).astype(jnp.bfloat16)


def solution(mesh):
    in_specs = (
        P(("attn", "ffn"), None),
        P(("attn", "ffn"), None, None),
        P(("attn", "ffn"), None, None),
        P(("attn", "ffn"), None),
        P(("attn", "ffn"), None),
        P(("attn", "ffn")),
        P(),
        P(None, "attn"),
        P("ffn", "attn"),
        P("attn"),
        P("attn", "ffn"),
        P("attn", "ffn"),
        P("ffn", "attn"),
    )
    out_specs = P("ffn", "attn")
    return jax.shard_map(local, mesh=mesh, in_specs=in_specs, out_specs=out_specs, check_vma=False)
```

profile of v0, /device:TPU:0, one launch (start us, length us, event | category | flops | bytes accessed | tf_op | source)
XLA Modules:
  0.0 648.2 jit_solution(10058126151798381865)
XLA Ops:
  6.5 1.0 copy.23
  7.6 0.7 iota_compare_fusion
  8.3 0.7 reshape.63
  9.1 1.7 fusion.17
  11.1 0.7 reshape.50
  11.8 1.5 fusion.4
  13.4 0.7 copy.18
  14.1 7.1 %all-to-all-start = ((bf16[4,16,512]{2,0,1:T(4,128)(2,1)}), bf16[4,16,512]{2,0,1:T(4,128)(2,1)S(1)}, u32[]{:S(2)}, u32[]{:S(2)}) async-start(bf16[4,16,512]{2,0,1:T(4,128)(2,1)} %copy.18), calls=%async_computation | async-start | bytes 131072 | tf_op jit(solution)/shard_map/all_to_all | solution.py:91
  21.3 7.6 %all-to-all-done = bf16[4,16,512]{2,0,1:T(4,128)(2,1)S(1)} async-done(((bf16[4,16,512]{2,0,1:T(4,128)(2,1)}), bf16[4,16,512]{2,0,1:T(4,128)(2,1)S(1)}, u32[]{:S(2)}, u32[]{:S(2)}) %all-to-all-start) | async-done | bytes 65568 | tf_op jit(solution)/shard_map/all_to_all | solution.py:91
  28.9 31.4 %all_gather.3 = bf16[512,512]{1,0:T(8,128)(2,1)S(1)} all-gather(bf16[64,512]{1,0:T(8,128)(2,1)S(1)} %all_to_all.14), channel_id=1, replica_groups=mesh['attn'=8,'ffn'=16] {'attn'}, dimensions={0}, use_global_device_ids=true | all-gather | bytes 589824 | tf_op jit(solution)/shard_map/all_gather | solution.py:93
  60.3 3.3 fusion.19
  63.5 7.6 %gather_fusion = f32[512,2048]{1,0:T(8,128)} fusion(f32[512,2048]{1,0:T(8,128)} %fusion.19, s32[1024]{0:T(1024)S(1)} %pad_clamp_fusion), kind=kCustom, calls=%fused_computation | custom fusion | bytes 8390656 | tf_op jit(solution)/shard_map/jit(_take)/gather | solution.py:97
  71.1 4.5 broadcast_select_fusion
  75.6 0.6 copy-done.5
  76.2 153.0 %all-reduce.4.cloned.1.call-done = f32[512,2048]{1,0:T(8,128)} async-done(((f32[512,2048]{1,0:T(8,128)}), f32[512,2048]{1,0:T(8,128)}) %all-reduce.4.cloned.1.call-update) | async-done | bytes 4194320 | tf_op jit(solution)/shard_map/psum | solution.py:102
  229.2 4.7 multiply_reduce_fusion
  233.9 19.0 %psum.29 = f32[512]{0:T(512)S(1)} all-reduce(f32[512]{0:T(512)S(1)} %get-tuple-element.7), channel_id=1, replica_groups=mesh['attn'=8,'ffn'=16] {'attn'}, use_global_device_ids=true, to_apply=%region_4.5 | all-reduce | flops 512 | bytes 4096 | tf_op jit(solution)/shard_map/psum | solution.py:67
  252.9 10.1 %fusion.16 = f32[512,1664]{1,0:T(8,128)} fusion(bf16[2048,1664]{1,0:T(8,128)(2,1)} %param.23, f32[512,2048]{1,0:T(8,128)} %get-tuple-element.8, f32[2048]{0:T(1024)S(1)} %convert_element_type.38, f32[512]{0:T(512)S(1)} %add_rsqrt_fusion), kind=kOutput, calls=%fused_computation.33 | convolution fusion | flops 3492806656 | bytes 14428160 | tf_op jit(solution)/shard_map/dot_general | solution.py:106
  262.9 8.8 %fusion.15 = f32[512,1664]{1,0:T(8,128)} fusion(bf16[2048,1664]{1,0:T(8,128)(2,1)} %param.24, f32[512,2048]{1,0:T(8,128)S(1)} %copy-done.2, f32[2048]{0:T(1024)S(1)} %convert_element_type.38, f32[512]{0:T(512)S(1)} %add_rsqrt_fusion), kind=kOutput, calls=%fused_computation.32 | convolution fusion | flops 3492806656 | bytes 14428160 | tf_op jit(solution)/shard_map/dot_general | solution.py:107
  271.7 0.2 reduce-scatter.2.cloned.1.call-start
  271.9 275.5 %all-reduce.6.cloned.1.call-done = (f32[512,1664]{1,0:T(8,128)}, f32[512,1664]{1,0:T(8,128)}) async-done(((f32[512,1664]{1,0:T(8,128)}, f32[512,1664]{1,0:T(8,128)}), (f32[512,1664]{1,0:T(8,128)}, f32[512,1664]{1,0:T(8,128)})) %all-reduce.6.cloned.1.call-update) | async-done | bytes 6815760 | tf_op jit(solution)/shard_map/psum | solution.py:108
  547.5 11.1 %fusion = f32[512,2048]{1,0:T(8,128)} fusion(bf16[1664,2048]{1,0:T(8,128)(2,1)} %param.25, f32[512,1664]{1,0:T(8,128)} %get-tuple-element.5, f32[512,1664]{1,0:T(8,128)} %get-tuple-element.6), kind=kOutput, calls=%fused_computation.6 | convolution fusion | flops 3494772736 | bytes 17825792 | tf_op jit(solution)/shard_map/dot_general | solution.py:111
  558.6 81.4 %reduce-scatter.2.cloned.1.call-done = f32[32,2048]{1,0:T(8,128)} async-done(((f32[512,2048]{1,0:T(8,128)}), f32[32,2048]{1,0:T(8,128)}) %reduce-scatter.2.cloned.1.call-update) | async-done | bytes 262160 | tf_op jit(solution)/shard_map/reduce_scatter | solution.py:110
  640.0 1.7 add_convert_fusion
  (27 shorter events, 0.6 us)
Async XLA Ops:
  6.5 53.7 %copy-start = (bf16[512,2048]{1,0:T(8,128)(2,1)S(1)}, bf16[512,2048]{1,0:T(8,128)(2,1)}, u32[]{:S(2)}) copy-start(bf16[512,2048]{1,0:T(8,128)(2,1)} %param.21) | copy-start | bytes 6291460
  6.5 14.7 %copy-start.4 = (s32[512]{0:T(512)S(1)}, s32[512]{0:T(512)}, u32[]{:S(2)}) copy-start(s32[512]{0:T(512)} %param.19) | copy-start | bytes 6148
  14.1 14.8 %all-to-all-start = ((bf16[4,16,512]{2,0,1:T(4,128)(2,1)}), bf16[4,16,512]{2,0,1:T(4,128)(2,1)S(1)}, u32[]{:S(2)}, u32[]{:S(2)}) async-start(bf16[4,16,512]{2,0,1:T(4,128)(2,1)} %copy.18), calls=%async_computation | async-start | bytes 131072 | tf_op jit(solution)/shard_map/all_to_all | solution.py:91
  21.2 208.0 %all-reduce.4.cloned.1.call-start = ((), (), s32[]{:S(2)}) async-start(), calls=%async_computation.2 | async-start | bytes 8388608 | tf_op jit(solution)/shard_map/psum | solution.py:102
  75.6 0.7 copy-start.5
  75.6 153.7 %copy-start.3 = (bf16[512,2048]{1,0:T(8,128)(2,1)S(1)}, bf16[512,2048]{1,0:T(8,128)(2,1)}, u32[]{:S(2)}) copy-start(bf16[512,2048]{1,0:T(8,128)(2,1)} %param.20) | copy-start | bytes 6291460
  75.6 471.9 %all-reduce.6.cloned.1.call-start = ((), (), s32[]{:S(2)}) async-start(), calls=%async_computation.4 | async-start | bytes 13631488 | tf_op jit(solution)/shard_map/psum | solution.py:108
  252.9 10.1 %copy-start.2 = (f32[512,2048]{1,0:T(8,128)S(1)}, f32[512,2048]{1,0:T(8,128)}, u32[]{:S(2)}) copy-start(f32[512,2048]{1,0:T(8,128)} %get-tuple-element.8) | copy-start | bytes 12582916
  271.7 368.3 %reduce-scatter.2.cloned.1.call-start = ((), (), s32[]{:S(2)}) async-start(), calls=%async_computation.3 | async-start | bytes 4456448 | tf_op jit(solution)/shard_map/reduce_scatter | solution.py:110
  547.5 94.2 %copy-start.1 = (bf16[512,2048]{1,0:T(8,128)(2,1)S(1)}, bf16[512,2048]{1,0:T(8,128)(2,1)}, u32[]{:S(2)}) copy-start(bf16[512,2048]{1,0:T(8,128)(2,1)} %param.21) | copy-start | bytes 6291460
Sparse Core Ops, SparseCore 0:
  75.7 153.4 all-reduce.3
  271.8 275.6 all-reduce.5
  558.7 81.1 reduce-scatter.1
where the time goes:
time: 649 us; the launch traced here: 648 us
  waiting for transfers between devices  517 us (80%)
  blocking collectives  50.3 us (8%)
  matrix products  36.6 us (6%)
  between operations  13.2 us (2%)
  other arithmetic  11.8 us (2%)
  local copies, waits for them, and re-layouts  11.4 us (2%)
  starting transfers between devices  7.42 us (1%)
    psum x1, waiting for transfers between devices, local(): gate_sum, up_sum = lax.psum((gate_part, up_part), 'attn')  276 us
    psum x1, waiting for transfers between devices, local(): summed = lax.psum(partial_value, 'ffn')  153 us
    reduce_scatter x1, waiting for transfers between devices, local(): lax.psum_scatter(jnp.dot(hidden, w_down, preferred_element_type=jnp.float...  81.4 us
    all_gather x1, blocking collectives, local(): lax.all_gather(exchanged, 'attn', axis=0, tiled=True)  31.4 us
    psum x1, blocking collectives, normalize(): squares = lax.psum(jnp.sum(row_state * row_state, axis=-1), 'attn')  19 us
  transfers between devices with their start and end apart: 4, of which 4 were waited for; matrix products, arithmetic and copies ran while one was open for 0% of the time, Pallas kernels for 0%

commit v1 on v0

v1 whole, which is shorter than its diff:
```python
import jax
import jax.numpy as jnp
from jax import lax
from jax.sharding import PartitionSpec as P

QUERY_HEADS = 64
KEY_VALUE_HEADS = 4
HEAD_SIZE = 128
SLOT_CAPACITY = 256

epsilon = 1e-05

ATTN, FFN = 8, 16
F32, BF16 = jnp.float32, jnp.bfloat16


def permute(value, move):
    pairs = []
    for a in range(ATTN):
        for f in range(FFN):
            to_a, to_f = move(a, f)
            pairs.append((a * FFN + f, to_a * FFN + to_f))
    return lax.ppermute(value, ("attn", "ffn"), pairs)


def to_core(value):
    return permute(value, lambda a, f: (a, f ^ 1))


def to_x_hi(value):
    return permute(value, lambda a, f: (a, f ^ 2))


def to_x_lo(value):
    return permute(value, lambda a, f: (a ^ 1, f))


def to_y(step):
    return lambda value: permute(value, lambda a, f: (a, (f + 4 * step) % FFN))


def to_z(step):
    return lambda value: permute(value, lambda a, f: ((a + 2 * step) % ATTN, f))


def ring_sum(blocks, to):
    up1 = to(1)(blocks[1:3].reshape((4,) + blocks.shape[2:])[1:3].astype(BF16))
    down1 = to(-1)(blocks[2:4].reshape((4,) + blocks.shape[2:])[1:3].astype(BF16))
    up2 = to(1)((blocks[1, 0] + up1[1].astype(F32)).astype(BF16))
    down2 = to(-1)((blocks[3, 1] + down1[0].astype(F32)).astype(BF16))
    first = blocks[0, 0] + up2.astype(F32) + down1[1].astype(F32)
    second = blocks[0, 1] + up1[0].astype(F32) + down2.astype(F32)
    return first, second


def ring_gather(own, to):
    before = to(1)(own)
    after = to(-1)(own)
    across_first = to(1)(before[0])
    across_second = to(-1)(after[1])
    return jnp.stack([own, after, jnp.stack([across_first, across_second]), before])


def sum_over_ffn(own_half, other_half):
    columns = own_half.shape[1]
    total = own_half + to_core(other_half.astype(BF16)).astype(F32)
    first, second = ring_sum(total.reshape(4, 2, -1, columns), to_y)
    return first + to_x_hi(second.astype(BF16)).astype(F32)


def attend(queries, slot_key_cache, slot_value_cache, fresh_token_key, fresh_token_value, lengths):
    request_slot_count = queries.shape[0]
    query_group_width = QUERY_HEADS // KEY_VALUE_HEADS
    query_head_rows = queries.reshape(
        request_slot_count, KEY_VALUE_HEADS, query_group_width, HEAD_SIZE
    )
    stored_keys = slot_key_cache.reshape(
        request_slot_count, SLOT_CAPACITY, KEY_VALUE_HEADS, HEAD_SIZE
    )
    stored_values = slot_value_cache.reshape(
        request_slot_count, SLOT_CAPACITY, KEY_VALUE_HEADS, HEAD_SIZE
    )
    current_key = fresh_token_key.reshape(request_slot_count, KEY_VALUE_HEADS, HEAD_SIZE)
    current_value = fresh_token_value.astype(F32).reshape(
        request_slot_count, KEY_VALUE_HEADS, HEAD_SIZE
    )
    factor = HEAD_SIZE ** (-0.5)
    scores = (
        jnp.einsum("sgqd,spgd->sgqp", query_head_rows, stored_keys, preferred_element_type=F32)
        * factor
    )
    own_score = (
        jnp.einsum("sgqd,sgd->sgq", query_head_rows, current_key, preferred_element_type=F32)
        * factor
    )
    live_mask = jnp.arange(SLOT_CAPACITY, dtype=jnp.int32)[None, :] < lengths[:, None]
    scores = jnp.where(live_mask[:, None, None, :], scores, -jnp.inf)
    highest = jnp.maximum(jnp.max(scores, axis=-1), own_score)
    weights = jnp.exp(scores - highest[..., None])
    own_weight = jnp.exp(own_score - highest)
    weight_sum = jnp.sum(weights, axis=-1) + own_weight
    own_low = own_weight.astype(BF16).astype(F32)
    combined = jnp.einsum(
        "sgqp,spgd->sgqd", weights.astype(BF16), stored_values, preferred_element_type=F32
    )
    combined = combined + own_low[..., None] * current_value[:, :, None, :]
    return (
        (combined / weight_sum[..., None])
        .reshape(request_slot_count, QUERY_HEADS * HEAD_SIZE)
        .astype(BF16)
    )


def local(
    queries,
    slot_key_cache,
    slot_value_cache,
    fresh_token_key,
    fresh_token_value,
    lengths,
    slot_of,
    residual,
    w_out,
    norm_gain,
    w_gate,
    w_up,
    w_down,
):
    a, f = lax.axis_index("attn"), lax.axis_index("ffn")
    z, x_lo = a // 2, a % 2
    y, x_hi, core = f // 4, (f // 2) % 2, f % 2
    slots = queries.shape[0]
    features = w_out.shape[0]
    width = w_out.shape[1]
    rows = residual.shape[0]
    share = rows // FFN
    batch = rows // ATTN
    width_total = width * ATTN

    attended = attend(
        queries, slot_key_cache, slot_value_cache, fresh_token_key, fresh_token_value, lengths
    )

    step = jnp.arange(FFN, dtype=jnp.int32)
    step_core, step_y, step_x = step // 8, (step // 2) % 4, step % 2
    partner = ((y + step_y) % 4) * 4 + (x_hi ^ step_x) * 2 + (core ^ step_core)

    parts = attended.reshape(slots, FFN, features).transpose(1, 0, 2)
    parts = jnp.take(parts, partner, axis=0).reshape(2, 4, 2, slots * features)
    parts = jnp.stack([parts[0], to_core(parts[1])])
    parts = jnp.stack([parts[:, :, 0], to_x_hi(parts[:, :, 1])])
    parts = jnp.stack(
        [parts[:, :, 0]] + [to_y(s)(parts[:, :, s]) for s in (1, 2, 3)]
    )
    parts = parts.reshape(2, FFN // 2, slots * features)
    parts = jnp.stack([parts, to_x_lo(parts)])
    parts = ring_gather(parts, to_z)
    held = parts.reshape(rows, features)

    wanted = (partner[:, None] * share + jnp.arange(share, dtype=jnp.int32)).reshape(rows)
    slot = jnp.take(slot_of, wanted)
    slot_a, slot_f, slot_i = slot // (FFN * slots), (slot // slots) % FFN, slot % slots
    place = (slot_a // 2 - z) % 4
    place = place * 2 + ((slot_a % 2) ^ x_lo)
    place = place * 4 + (y - slot_f // 4) % 4
    place = place * 2 + (((slot_f // 2) % 2) ^ x_hi)
    place = place * 2 + ((slot_f % 2) ^ core)
    place = place * slots + slot_i
    choice = (place[:, None] == jnp.arange(rows, dtype=jnp.int32)[None, :]).astype(BF16)
    ordered = jnp.dot(choice, held, preferred_element_type=F32).astype(BF16)

    half = rows // 2
    summed = sum_over_ffn(
        jnp.dot(ordered[:half], w_out, preferred_element_type=F32),
        jnp.dot(ordered[half:], w_out, preferred_element_type=F32),
    )
    kept = lax.dynamic_slice_in_dim(residual, f * share, share, 0).astype(F32)
    hidden_state = kept + summed

    squares = jnp.sum(hidden_state * hidden_state, axis=-1)
    squares = squares + to_x_lo(squares)
    squares = squares + to_z(1)(squares) + to_z(2)(squares) + to_z(3)(squares)
    gain = norm_gain.astype(F32)
    normed = (
        hidden_state * lax.rsqrt(squares / width_total + epsilon)[:, None] * gain
    ).astype(BF16)

    normed = jnp.stack([normed, to_x_hi(normed)])
    normed = ring_gather(normed, to_y)
    normed = jnp.stack([normed, to_core(normed)])

    ahead = jnp.arange(ATTN, dtype=jnp.int32)
    order = ((z + ahead // 2) % 4) * 2 + (x_lo ^ (ahead % 2))
    back = ((ahead // 2 - z) % 4) * 2 + (x_lo ^ (ahead % 2))
    normed = jnp.take(normed.reshape(ATTN, batch, width), order, axis=0).reshape(rows, width)

    up = jnp.dot(normed, w_up, preferred_element_type=F32).reshape(4, 2, batch, -1)
    gate = jnp.dot(normed, w_gate, preferred_element_type=F32).reshape(4, 2, batch, -1)
    units = w_up.shape[1]
    up = up[:, 0] + to_x_lo(up[:, 1].astype(BF16)).astype(F32)
    gate, gate_across = ring_sum(gate, to_z)
    gate = gate + to_x_lo(gate_across.astype(BF16)).astype(F32)
    up = jnp.concatenate(ring_sum(up.reshape(4, 2, batch // 2, units), to_z), axis=0)
    hidden = (jax.nn.silu(gate) * up).astype(BF16)

    cut = 128 * (units // 256)
    left, right = hidden[:, :cut], hidden[:, cut:]
    left = ring_gather(jnp.stack([left, to_x_lo(left)]), to_z)
    right = ring_gather(right.reshape(2, batch // 2, -1), to_z).reshape(4, batch, -1)
    right = jnp.stack([right, to_x_lo(right)], axis=1)
    hidden = jnp.concatenate([left, right], axis=-1).reshape(ATTN, batch, units)
    hidden = jnp.take(hidden, back, axis=0).reshape(rows, units)

    down_out = sum_over_ffn(
        jnp.dot(hidden[:half], w_down, preferred_element_type=F32),
        jnp.dot(hidden[half:], w_down, preferred_element_type=F32),
    )
    return (hidden_state + down_out).astype(BF16)


def solution(mesh):
    in_specs = (
        P(("attn", "ffn"), None),
        P(("attn", "ffn"), None, None),
        P(("attn", "ffn"), None, None),
        P(("attn", "ffn"), None),
        P(("attn", "ffn"), None),
        P(("attn", "ffn")),
        P(),
        P(None, "attn"),
        P("ffn", "attn"),
        P("attn"),
        P("attn", "ffn"),
        P("attn", "ffn"),
        P("ffn", "attn"),
    )
    out_specs = P("ffn", "attn")
    return jax.shard_map(local, mesh=mesh, in_specs=in_specs, out_specs=out_specs, check_vma=False)
```

time: 649 us -> 240 us (0.37)
  waiting for transfers between devices: 517 us -> 119 us
  starting transfers between devices: 7.42 us -> 71.5 us
  blocking collectives: 50.3 us -> 0 us
  between operations: 13.2 us -> 0.69 us
  matrix products: 36.6 us -> 26.6 us
    psum x2 -> x0, waiting for transfers between devices: 429 us -> none  [the longest x1 276 us: local(): gate_sum, up_sum = lax.psum((gate_part, up_part), 'attn')]
    ppermute x0 -> x52, waiting for transfers between devices: none -> 119 us  [permute(): return lax.ppermute(value, ('attn', 'ffn'), pairs)]
    reduce_scatter x1 -> x0, waiting for transfers between devices: 81.4 us -> none  [local(): lax.psum_scatter(jnp.dot(hidden, w_down, preferred_element_type=jnp.float...]
    ppermute x0 -> x52, starting transfers between devices: none -> 71.5 us  [permute(): return lax.ppermute(value, ('attn', 'ffn'), pairs)]
    all_gather x1 -> x0, blocking collectives: 31.4 us -> none  [local(): lax.all_gather(exchanged, 'attn', axis=0, tiled=True)]
    psum x1 -> x0, blocking collectives: 19 us -> none  [normalize(): squares = lax.psum(jnp.sum(row_state * row_state, axis=-1), 'attn')]
    dot_general x5 -> x8, matrix products: 34.7 us -> 24.7 us  [the longest x1 6.92 us: local(): jnp.dot(normed, w_up, preferred_element_type=F32).reshape(4, 2, batch, -1)]
    all_to_all x1 -> x0, waiting for transfers between devices: 7.57 us -> none  [local(): lax.all_to_all(attended, 'ffn', split_axis=1, concat_axis=0, tiled=True)]
  transfers between devices with their start and end apart: 4 -> 52, of which waited for: 4 -> 37; matrix products, arithmetic and copies ran while one was open for 0% -> 5% of each run, Pallas kernels for 0% -> 0%
where the time goes in v1:
time: 240 us; the launch traced here: 239 us
  waiting for transfers between devices  119 us (50%)
  starting transfers between devices  71.5 us (30%)
  matrix products  26.6 us (11%)
  local copies, waits for them, and re-layouts  12.3 us (5%)
  other arithmetic  8.84 us (4%)
    ppermute x52, waiting for transfers between devices, permute(): return lax.ppermute(value, ('attn', 'ffn'), pairs)  119 us
    ppermute x52, starting transfers between devices, permute(): return lax.ppermute(value, ('attn', 'ffn'), pairs)  71.5 us
    dot_general x1, matrix products, local(): jnp.dot(normed, w_up, preferred_element_type=F32).reshape(4, 2, batch, -1)  6.92 us
    dot_general x1, matrix products, local(): jnp.dot(normed, w_gate, preferred_element_type=F32).reshape(4, 2, batch, -1)  6.88 us
    dot_general x1, matrix products, local(): jnp.dot(hidden[half:], w_down, preferred_element_type=F32)  5.27 us
  transfers between devices with their start and end apart: 52, of which 37 were waited for; matrix products, arithmetic and copies ran while one was open for 5% of the time, Pallas kernels for 0%

profile of v1, /device:TPU:0, one launch (start us, length us, event | category | flops | bytes accessed | tf_op | source)
XLA Modules:
  0.0 239.4 jit_solution(18161997682231530019)
XLA Ops:
  19.8 3.5 %collective-permute-done.3 = bf16[2,2,2048]{2,1,0:T(2,128)(2,1)S(1)} collective-permute-done((bf16[2,2,2048]{2,1,0:T(2,128)(2,1)S(1)}, bf16[2,2,2048]{2,1,0:T(2,128)(2,1)S(1)}, u32[]{:S(2)}, u32[]{:S(2)}) %collective-permute-start.3) | collective-permute-done | bytes 16416 | tf_op jit(solution)/shard_map/ppermute | solution.py:23
  28.3 4.1 %collective-permute-start.6 = (bf16[2,2,8,2048]{3,2,1,0:T(8,128)(2,1)S(1)}, bf16[2,2,8,2048]{3,2,1,0:T(8,128)(2,1)S(1)}, u32[]{:S(2)}, u32[]{:S(2)}) collective-permute-start(bf16[2,2,8,2048]{3,2,1,0:T(8,128)(2,1)S(1)} %get-tuple-element.41), channel_id=1, source_target_pairs={{0,96},{1,97},{2,98},{3,99},{4,100},{5,101},{6,102},{7,103},{8,104... | collective-permute-start | bytes 393224 | tf_op jit(solution)/shard_map/ppermute | solution.py:23
  32.5 3.5 %gather_fusion = s32[512]{0:T(512)S(1)} fusion(s32[512]{0:T(512)S(1)} %copy-done.2, s32[1024]{0:T(1024)S(1)} %pad_clamp_fusion.3), kind=kCustom, calls=%fused_computation | custom fusion | bytes 6144 | tf_op jit(solution)/shard_map/jit(_take)/gather | solution.py:161
  39.4 3.5 %collective-permute-done.7 = bf16[2,2,8,2048]{3,2,1,0:T(8,128)(2,1)S(1)} collective-permute-done((bf16[2,2,8,2048]{3,2,1,0:T(8,128)(2,1)S(1)}, bf16[2,2,8,2048]{3,2,1,0:T(8,128)(2,1)S(1)}, u32[]{:S(2)}, u32[]{:S(2)}) %collective-permute-start.7) | collective-permute-done | bytes 131104 | tf_op jit(solution)/shard_map/ppermute | solution.py:23
  43.0 5.4 %collective-permute-done.8 = bf16[2,8,2048]{2,1,0:T(8,128)(2,1)S(1)} collective-permute-done((bf16[2,8,2048]{2,1,0:T(8,128)(2,1)S(1)}, bf16[2,8,2048]{2,1,0:T(8,128)(2,1)S(1)}, u32[]{:S(2)}, u32[]{:S(2)}) %collective-permute-start.8) | collective-permute-done | bytes 65568 | tf_op jit(solution)/shard_map/ppermute | solution.py:23
  55.8 6.3 %collective-permute-done.13 = bf16[2,32,2048]{2,1,0:T(8,128)(2,1)S(1)} collective-permute-done((bf16[2,32,2048]{2,1,0:T(8,128)(2,1)S(1)}, bf16[2,32,2048]{2,1,0:T(8,128)(2,1)S(1)}, u32[]{:S(2)}, u32[]{:S(2)}) %collective-permute-start.13) | collective-permute-done | bytes 262176 | tf_op jit(solution)/shard_map/ppermute | solution.py:23
  63.8 3.4 %collective-permute-done.14 = bf16[32,2048]{1,0:T(8,128)(2,1)S(1)} collective-permute-done((bf16[32,2048]{1,0:T(8,128)(2,1)S(1)}, bf16[32,2048]{1,0:T(8,128)(2,1)S(1)}, u32[]{:S(2)}, u32[]{:S(2)}) %collective-permute-start.14) | collective-permute-done | bytes 131104 | tf_op jit(solution)/shard_map/ppermute | solution.py:23
  70.3 3.5 %collective-permute-done.15 = bf16[32,2048]{1,0:T(8,128)(2,1)S(1)} collective-permute-done((bf16[32,2048]{1,0:T(8,128)(2,1)S(1)}, bf16[32,2048]{1,0:T(8,128)(2,1)S(1)}, u32[]{:S(2)}, u32[]{:S(2)}) %collective-permute-start.15) | collective-permute-done | bytes 131104 | tf_op jit(solution)/shard_map/ppermute | solution.py:23
  88.4 5.8 %collective-permute-done.20 = bf16[32,2048]{1,0:T(8,128)(2,1)S(1)} collective-permute-done((bf16[32,2048]{1,0:T(8,128)(2,1)S(1)}, bf16[32,2048]{1,0:T(8,128)(2,1)S(1)}, u32[]{:S(2)}, u32[]{:S(2)}) %collective-permute-start.20) | collective-permute-done | bytes 131104 | tf_op jit(solution)/shard_map/ppermute | solution.py:23
  96.5 4.3 %collective-permute-done.21 = bf16[2,32,2048]{2,1,0:T(8,128)(2,1)S(1)} collective-permute-done((bf16[2,32,2048]{2,1,0:T(8,128)(2,1)S(1)}, bf16[2,32,2048]{2,1,0:T(8,128)(2,1)S(1)}, u32[]{:S(2)}, u32[]{:S(2)}) %collective-permute-start.21) | collective-permute-done | bytes 262176 | tf_op jit(solution)/shard_map/ppermute | solution.py:23
  106.5 3.7 %collective-permute-done.23 = bf16[32,2048]{1,0:T(8,128)(2,1)S(1)} collective-permute-done((bf16[32,2048]{1,0:T(8,128)(2,1)S(1)}, bf16[32,2048]{1,0:T(8,128)(2,1)S(1)}, u32[]{:S(2)}, u32[]{:S(2)}) %collective-permute-start.23) | collective-permute-done | bytes 131104 | tf_op jit(solution)/shard_map/ppermute | solution.py:23
  116.9 6.9 %fusion = f32[4,2,64,1664]{3,2,1,0:T(8,128)S(1)} fusion(bf16[2048,1664]{1,0:T(8,128)(2,1)} %param.24, bf16[4,2,64,2048]{3,2,1,0:T(8,128)(2,1)S(1)} %bitcast.365, pred[4,2]{1,0:T(4,128)(4,1)S(1)} %compare_and_fusion), kind=kOutput, calls=%fused_computation.4 | convolution fusion | flops 3490709504 | bytes 12320776 | tf_op jit(solution)/shard_map/dot_general | solution.py:197
  124.9 6.9 %fusion.153 = (bf16[512,1664]{1,0:T(8,128)(2,1)S(1)}, f32[512,1664]{1,0:T(8,128)S(1)}) fusion(bf16[512,2048]{1,0:T(8,128)(2,1)S(1)} %bitcast_select_fusion, bf16[2048,1664]{1,0:T(8,128)(2,1)} %param.23), kind=kOutput, calls=%fused_computation.359 | convolution fusion | flops 3490512896 | bytes 14024704 | tf_op jit(solution)/shard_map/dot_general | solution.py:198
  131.8 13.3 %collective-permute-done.31 = bf16[4,64,1664]{2,1,0:T(8,128)(2,1)S(1)} collective-permute-done((bf16[4,64,1664]{2,1,0:T(8,128)(2,1)S(1)}, bf16[4,64,1664]{2,1,0:T(8,128)(2,1)S(1)}, u32[]{:S(2)}, u32[]{:S(2)}) %collective-permute-start.31) | collective-permute-done | bytes 852000 | tf_op jit(solution)/shard_map/ppermute | solution.py:23
  150.9 3.9 %collective-permute-done.32 = bf16[2,32,1664]{2,1,0:T(8,128)(2,1)S(1)} collective-permute-done((bf16[2,32,1664]{2,1,0:T(8,128)(2,1)S(1)}, bf16[2,32,1664]{2,1,0:T(8,128)(2,1)S(1)}, u32[]{:S(2)}, u32[]{:S(2)}) %collective-permute-start.32) | collective-permute-done | bytes 213024 | tf_op jit(solution)/shard_map/ppermute | solution.py:23
  154.9 5.0 %collective-permute-done.28 = bf16[2,64,1664]{2,1,0:T(8,128)(2,1)S(1)} collective-permute-done((bf16[2,64,1664]{2,1,0:T(8,128)(2,1)S(1)}, bf16[2,64,1664]{2,1,0:T(8,128)(2,1)S(1)}, u32[]{:S(2)}, u32[]{:S(2)}) %collective-permute-start.28) | collective-permute-done | bytes 426016 | tf_op jit(solution)/shard_map/ppermute | solution.py:23
  159.9 3.8 %collective-permute-start.29 = (bf16[64,1664]{1,0:T(8,128)(2,1)S(1)}, bf16[64,1664]{1,0:T(8,128)(2,1)S(1)}, u32[]{:S(2)}, u32[]{:S(2)}) collective-permute-start(bf16[64,1664]{1,0:T(8,128)(2,1)S(1)} %fusion.16), channel_id=1, source_target_pairs={{0,96},{1,97},{2,98},{3,99},{4,100},{5,101},{6,102},{7,103},{8,104... | collective-permute-start | bytes 638984 | tf_op jit(solution)/shard_map/ppermute | solution.py:23
  164.5 3.7 %collective-permute-start.35 = (bf16[32,1664]{1,0:T(8,128)(2,1)S(1)}, bf16[32,1664]{1,0:T(8,128)(2,1)S(1)}, u32[]{:S(2)}, u32[]{:S(2)}) collective-permute-start(bf16[32,1664]{1,0:T(8,128)(2,1)S(1)} %get-tuple-element.18), channel_id=1, source_target_pairs={{0,96},{1,97},{2,98},{3,99},{4,100},{5,101},{6,102},{7,103},{8,104... | collective-permute-start | bytes 319496 | tf_op jit(solution)/shard_map/ppermute | solution.py:23
  170.6 3.7 %collective-permute-done.30 = bf16[64,1664]{1,0:T(8,128)(2,1)S(1)} collective-permute-done((bf16[64,1664]{1,0:T(8,128)(2,1)S(1)}, bf16[64,1664]{1,0:T(8,128)(2,1)S(1)}, u32[]{:S(2)}, u32[]{:S(2)}) %collective-permute-start.30) | collective-permute-done | bytes 213024 | tf_op jit(solution)/shard_map/ppermute | solution.py:23
  198.5 3.7 %collective-permute-done.39 = bf16[64,768]{1,0:T(8,128)(2,1)S(1)} collective-permute-done((bf16[64,768]{1,0:T(8,128)(2,1)S(1)}, bf16[64,768]{1,0:T(8,128)(2,1)S(1)}, u32[]{:S(2)}, u32[]{:S(2)}) %collective-permute-start.39) | collective-permute-done | bytes 98336 | tf_op jit(solution)/shard_map/ppermute | solution.py:23
  206.2 5.3 %convolution_convert_fusion = bf16[256,2048]{1,0:T(8,128)(2,1)S(1)} fusion(bf16[256,1664]{1,0:T(8,128)(2,1)S(1)} %bitcast.383, bf16[1664,2048]{1,0:T(8,128)(2,1)} %param.25), kind=kOutput, calls=%fused_computation.6 | convolution fusion | flops 1745354752 | bytes 8716288 | tf_op jit(solution)/shard_map/dot_general | solution.py:216
  218.4 6.3 %collective-permute-done.49 = bf16[2,32,2048]{2,1,0:T(8,128)(2,1)S(1)} collective-permute-done((bf16[2,32,2048]{2,1,0:T(8,128)(2,1)S(1)}, bf16[2,32,2048]{2,1,0:T(8,128)(2,1)S(1)}, u32[]{:S(2)}, u32[]{:S(2)}) %collective-permute-start.49) | collective-permute-done | bytes 262176 | tf_op jit(solution)/shard_map/ppermute | solution.py:23
  226.4 3.5 %collective-permute-done.50 = bf16[32,2048]{1,0:T(8,128)(2,1)S(1)} collective-permute-done((bf16[32,2048]{1,0:T(8,128)(2,1)S(1)}, bf16[32,2048]{1,0:T(8,128)(2,1)S(1)}, u32[]{:S(2)}, u32[]{:S(2)}) %collective-permute-start.50) | collective-permute-done | bytes 131104 | tf_op jit(solution)/shard_map/ppermute | solution.py:23
  232.4 4.0 %collective-permute-done.51 = bf16[32,2048]{1,0:T(8,128)(2,1)S(1)} collective-permute-done((bf16[32,2048]{1,0:T(8,128)(2,1)S(1)}, bf16[32,2048]{1,0:T(8,128)(2,1)S(1)}, u32[]{:S(2)}, u32[]{:S(2)}) %collective-permute-start.51) | collective-permute-done | bytes 131104 | tf_op jit(solution)/shard_map/ppermute | solution.py:23
  (202 shorter events, 121.6 us)
Async XLA Ops:
  28.3 7.8 %collective-permute-start.6 = (bf16[2,2,8,2048]{3,2,1,0:T(8,128)(2,1)S(1)}, bf16[2,2,8,2048]{3,2,1,0:T(8,128)(2,1)S(1)}, u32[]{:S(2)}, u32[]{:S(2)}) collective-permute-start(bf16[2,2,8,2048]{3,2,1,0:T(8,128)(2,1)S(1)} %get-tuple-element.41), channel_id=1, source_target_pairs={{0,96},{1,97},{2,98},{3,99},{4,100},{5,101},{6,102},{7,103},{8,104... | collective-permute-start | bytes 393224 | tf_op jit(solution)/shard_map/ppermute | solution.py:23
  36.0 6.9 %collective-permute-start.7 = (bf16[2,2,8,2048]{3,2,1,0:T(8,128)(2,1)S(1)}, bf16[2,2,8,2048]{3,2,1,0:T(8,128)(2,1)S(1)}, u32[]{:S(2)}, u32[]{:S(2)}) collective-permute-start(bf16[2,2,8,2048]{3,2,1,0:T(8,128)(2,1)S(1)} %get-tuple-element.41), channel_id=1, source_target_pairs={{0,32},{1,33},{2,34},{3,35},{4,36},{5,37},{6,38},{7,39},{8,40},{9,... | collective-permute-start | bytes 393224 | tf_op jit(solution)/shard_map/ppermute | solution.py:23
  36.1 6.9 %collective-permute-start.9 = (bf16[2,8,2048]{2,1,0:T(8,128)(2,1)S(1)}, bf16[2,8,2048]{2,1,0:T(8,128)(2,1)S(1)}, u32[]{:S(2)}, u32[]{:S(2)}) collective-permute-start(bf16[2,8,2048]{2,1,0:T(8,128)(2,1)S(1)} %slice_bitcast_fusion.37), channel_id=1, source_target_pairs={{0,96},{1,97},{2,98},{3,99},{4,100},{5,101},{6,102},{7,103},{8,104... | collective-permute-start | bytes 196616 | tf_op jit(solution)/shard_map/ppermute | solution.py:23
  53.7 8.4 %collective-permute-start.13 = (bf16[2,32,2048]{2,1,0:T(8,128)(2,1)S(1)}, bf16[2,32,2048]{2,1,0:T(8,128)(2,1)S(1)}, u32[]{:S(2)}, u32[]{:S(2)}) collective-permute-start(bf16[2,32,2048]{2,1,0:T(8,128)(2,1)S(1)} %bitcast.405), channel_id=1, source_target_pairs={{0,12},{1,13},{2,14},{3,15},{4,0},{5,1},{6,2},{7,3},{8,4},{9,5},{1... | collective-permute-start | bytes 786440 | tf_op jit(solution)/shard_map/ppermute | solution.py:23
  54.1 9.6 %collective-permute-start.11 = (bf16[2,32,2048]{2,1,0:T(8,128)(2,1)S(1)}, bf16[2,32,2048]{2,1,0:T(8,128)(2,1)S(1)}, u32[]{:S(2)}, u32[]{:S(2)}) collective-permute-start(bf16[2,32,2048]{2,1,0:T(8,128)(2,1)S(1)} %bitcast.403), channel_id=1, source_target_pairs={{0,4},{1,5},{2,6},{3,7},{4,8},{5,9},{6,10},{7,11},{8,12},{9,13},{1... | collective-permute-start | bytes 786440 | tf_op jit(solution)/shard_map/ppermute | solution.py:23
  87.6 6.6 %collective-permute-start.20 = (bf16[32,2048]{1,0:T(8,128)(2,1)S(1)}, bf16[32,2048]{1,0:T(8,128)(2,1)S(1)}, u32[]{:S(2)}, u32[]{:S(2)}) collective-permute-start(bf16[32,2048]{1,0:T(8,128)(2,1)S(1)} %multiply_convert_fusion), channel_id=1, source_target_pairs={{0,2},{1,3},{2,0},{3,1},{4,6},{5,7},{6,4},{7,5},{8,10},{9,11},{10,... | collective-permute-start | bytes 393224 | tf_op jit(solution)/shard_map/ppermute | solution.py:23
  94.2 6.6 %collective-permute-start.21 = (bf16[2,32,2048]{2,1,0:T(8,128)(2,1)S(1)}, bf16[2,32,2048]{2,1,0:T(8,128)(2,1)S(1)}, u32[]{:S(2)}, u32[]{:S(2)}) collective-permute-start(bf16[2,32,2048]{2,1,0:T(8,128)(2,1)S(1)} %get-tuple-element.32), channel_id=1, source_target_pairs={{0,12},{1,13},{2,14},{3,15},{4,0},{5,1},{6,2},{7,3},{8,4},{9,5},{1... | collective-permute-start | bytes 786440 | tf_op jit(solution)/shard_map/ppermute | solution.py:23
  96.1 7.9 %collective-permute-start.22 = (bf16[2,32,2048]{2,1,0:T(8,128)(2,1)S(1)}, bf16[2,32,2048]{2,1,0:T(8,128)(2,1)S(1)}, u32[]{:S(2)}, u32[]{:S(2)}) collective-permute-start(bf16[2,32,2048]{2,1,0:T(8,128)(2,1)S(1)} %get-tuple-element.32), channel_id=1, source_target_pairs={{0,4},{1,5},{2,6},{3,7},{4,8},{5,9},{6,10},{7,11},{8,12},{9,13},{1... | collective-permute-start | bytes 786440 | tf_op jit(solution)/shard_map/ppermute | solution.py:23
  124.0 21.1 %collective-permute-start.31 = (bf16[4,64,1664]{2,1,0:T(8,128)(2,1)S(1)}, bf16[4,64,1664]{2,1,0:T(8,128)(2,1)S(1)}, u32[]{:S(2)}, u32[]{:S(2)}) collective-permute-start(bf16[4,64,1664]{2,1,0:T(8,128)(2,1)S(1)} %fusion.13), channel_id=1, source_target_pairs={{0,16},{1,17},{2,18},{3,19},{4,20},{5,21},{6,22},{7,23},{8,24},{9,... | collective-permute-start | bytes 2555912 | tf_op jit(solution)/shard_map/ppermute | solution.py:23
  145.3 9.5 %collective-permute-start.32 = (bf16[2,32,1664]{2,1,0:T(8,128)(2,1)S(1)}, bf16[2,32,1664]{2,1,0:T(8,128)(2,1)S(1)}, u32[]{:S(2)}, u32[]{:S(2)}) collective-permute-start(bf16[2,32,1664]{2,1,0:T(8,128)(2,1)S(1)} %slice.363), channel_id=1, source_target_pairs={{0,32},{1,33},{2,34},{3,35},{4,36},{5,37},{6,38},{7,39},{8,40},{9,... | collective-permute-start | bytes 638984 | tf_op jit(solution)/shard_map/ppermute | solution.py:23
  146.3 22.0 %collective-permute-start.26 = (bf16[2,64,1664]{2,1,0:T(8,128)(2,1)S(1)}, bf16[2,64,1664]{2,1,0:T(8,128)(2,1)S(1)}, u32[]{:S(2)}, u32[]{:S(2)}) collective-permute-start(bf16[2,64,1664]{2,1,0:T(8,128)(2,1)S(1)} %bitcast.396), channel_id=1, source_target_pairs={{0,32},{1,33},{2,34},{3,35},{4,36},{5,37},{6,38},{7,39},{8,40},{9,... | collective-permute-start | bytes 1277960 | tf_op jit(solution)/shard_map/ppermute | solution.py:23
  146.7 13.1 %collective-permute-start.28 = (bf16[2,64,1664]{2,1,0:T(8,128)(2,1)S(1)}, bf16[2,64,1664]{2,1,0:T(8,128)(2,1)S(1)}, u32[]{:S(2)}, u32[]{:S(2)}) collective-permute-start(bf16[2,64,1664]{2,1,0:T(8,128)(2,1)S(1)} %bitcast.397), channel_id=1, source_target_pairs={{0,96},{1,97},{2,98},{3,99},{4,100},{5,101},{6,102},{7,103},{8,104... | collective-permute-start | bytes 1277960 | tf_op jit(solution)/shard_map/ppermute | solution.py:23
  149.6 14.8 %collective-permute-start.34 = (bf16[2,32,1664]{2,1,0:T(8,128)(2,1)S(1)}, bf16[2,32,1664]{2,1,0:T(8,128)(2,1)S(1)}, u32[]{:S(2)}, u32[]{:S(2)}) collective-permute-start(bf16[2,32,1664]{2,1,0:T(8,128)(2,1)S(1)} %slice.366), channel_id=1, source_target_pairs={{0,96},{1,97},{2,98},{3,99},{4,100},{5,101},{6,102},{7,103},{8,104... | collective-permute-start | bytes 638984 | tf_op jit(solution)/shard_map/ppermute | solution.py:23
  154.8 9.7 %collective-permute-start.33 = (bf16[32,1664]{1,0:T(8,128)(2,1)S(1)}, bf16[32,1664]{1,0:T(8,128)(2,1)S(1)}, u32[]{:S(2)}, u32[]{:S(2)}) collective-permute-start(bf16[32,1664]{1,0:T(8,128)(2,1)S(1)} %fusion.61), channel_id=1, source_target_pairs={{0,32},{1,33},{2,34},{3,35},{4,36},{5,37},{6,38},{7,39},{8,40},{9,... | collective-permute-start | bytes 319496 | tf_op jit(solution)/shard_map/ppermute | solution.py:23
  159.9 8.4 %collective-permute-start.29 = (bf16[64,1664]{1,0:T(8,128)(2,1)S(1)}, bf16[64,1664]{1,0:T(8,128)(2,1)S(1)}, u32[]{:S(2)}, u32[]{:S(2)}) collective-permute-start(bf16[64,1664]{1,0:T(8,128)(2,1)S(1)} %fusion.16), channel_id=1, source_target_pairs={{0,96},{1,97},{2,98},{3,99},{4,100},{5,101},{6,102},{7,103},{8,104... | collective-permute-start | bytes 638984 | tf_op jit(solution)/shard_map/ppermute | solution.py:23
  169.0 7.3 %collective-permute-start.27 = (bf16[64,1664]{1,0:T(8,128)(2,1)S(1)}, bf16[64,1664]{1,0:T(8,128)(2,1)S(1)}, u32[]{:S(2)}, u32[]{:S(2)}) collective-permute-start(bf16[64,1664]{1,0:T(8,128)(2,1)S(1)} %get-tuple-element.11), channel_id=1, source_target_pairs={{0,32},{1,33},{2,34},{3,35},{4,36},{5,37},{6,38},{7,39},{8,40},{9,... | collective-permute-start | bytes 638984 | tf_op jit(solution)/shard_map/ppermute | solution.py:23
  176.5 9.3 %collective-permute-start.42 = (bf16[2,32,896]{2,1,0:T(8,128)(2,1)S(1)}, bf16[2,32,896]{2,1,0:T(8,128)(2,1)S(1)}, u32[]{:S(2)}, u32[]{:S(2)}) collective-permute-start(bf16[2,32,896]{2,1,0:T(8,128)(2,1)S(1)} %bitcast.411), channel_id=1, source_target_pairs={{0,32},{1,33},{2,34},{3,35},{4,36},{5,37},{6,38},{7,39},{8,40},{9,... | collective-permute-start | bytes 344072 | tf_op jit(solution)/shard_map/ppermute | solution.py:23
  182.4 6.9 %collective-permute-start.44 = (bf16[32,896]{1,0:T(8,128)(2,1)S(1)}, bf16[32,896]{1,0:T(8,128)(2,1)S(1)}, u32[]{:S(2)}, u32[]{:S(2)}) collective-permute-start(bf16[32,896]{1,0:T(8,128)(2,1)S(1)} %slice_bitcast_fusion.39), channel_id=1, source_target_pairs={{0,96},{1,97},{2,98},{3,99},{4,100},{5,101},{6,102},{7,103},{8,104... | collective-permute-start | bytes 172040 | tf_op jit(solution)/shard_map/ppermute | solution.py:23
  185.9 10.3 %collective-permute-start.38 = (bf16[2,64,768]{2,1,0:T(8,128)(2,1)S(1)}, bf16[2,64,768]{2,1,0:T(8,128)(2,1)S(1)}, u32[]{:S(2)}, u32[]{:S(2)}) collective-permute-start(bf16[2,64,768]{2,1,0:T(8,128)(2,1)S(1)} %get-tuple-element.39), channel_id=1, source_target_pairs={{0,32},{1,33},{2,34},{3,35},{4,36},{5,37},{6,38},{7,39},{8,40},{9,... | collective-permute-start | bytes 589832 | tf_op jit(solution)/shard_map/ppermute | solution.py:23
  186.0 7.1 %collective-permute-start.37 = (bf16[2,64,768]{2,1,0:T(8,128)(2,1)S(1)}, bf16[2,64,768]{2,1,0:T(8,128)(2,1)S(1)}, u32[]{:S(2)}, u32[]{:S(2)}) collective-permute-start(bf16[2,64,768]{2,1,0:T(8,128)(2,1)S(1)} %get-tuple-element.39), channel_id=1, source_target_pairs={{0,96},{1,97},{2,98},{3,99},{4,100},{5,101},{6,102},{7,103},{8,104... | collective-permute-start | bytes 589832 | tf_op jit(solution)/shard_map/ppermute | solution.py:23
  191.4 10.8 %collective-permute-start.45 = (bf16[4,64,896]{2,1,0:T(8,128)(2,1)S(1)}, bf16[4,64,896]{2,1,0:T(8,128)(2,1)S(1)}, u32[]{:S(2)}, u32[]{:S(2)}) collective-permute-start(bf16[4,64,896]{2,1,0:T(8,128)(2,1)S(1)} %pad_maximum_fusion.3), channel_id=1, source_target_pairs={{0,16},{1,17},{2,18},{3,19},{4,20},{5,21},{6,22},{7,23},{8,24},{9,... | collective-permute-start | bytes 1376264 | tf_op jit(solution)/shard_map/ppermute | solution.py:23
  216.3 8.4 %collective-permute-start.49 = (bf16[2,32,2048]{2,1,0:T(8,128)(2,1)S(1)}, bf16[2,32,2048]{2,1,0:T(8,128)(2,1)S(1)}, u32[]{:S(2)}, u32[]{:S(2)}) collective-permute-start(bf16[2,32,2048]{2,1,0:T(8,128)(2,1)S(1)} %bitcast.406), channel_id=1, source_target_pairs={{0,12},{1,13},{2,14},{3,15},{4,0},{5,1},{6,2},{7,3},{8,4},{9,5},{1... | collective-permute-start | bytes 786440 | tf_op jit(solution)/shard_map/ppermute | solution.py:23
  216.4 9.9 %collective-permute-start.47 = (bf16[2,32,2048]{2,1,0:T(8,128)(2,1)S(1)}, bf16[2,32,2048]{2,1,0:T(8,128)(2,1)S(1)}, u32[]{:S(2)}, u32[]{:S(2)}) collective-permute-start(bf16[2,32,2048]{2,1,0:T(8,128)(2,1)S(1)} %bitcast.404), channel_id=1, source_target_pairs={{0,4},{1,5},{2,6},{3,7},{4,8},{5,9},{6,10},{7,11},{8,12},{9,13},{1... | collective-permute-start | bytes 786440 | tf_op jit(solution)/shard_map/ppermute | solution.py:23
  229.9 6.6 %collective-permute-start.51 = (bf16[32,2048]{1,0:T(8,128)(2,1)S(1)}, bf16[32,2048]{1,0:T(8,128)(2,1)S(1)}, u32[]{:S(2)}, u32[]{:S(2)}) collective-permute-start(bf16[32,2048]{1,0:T(8,128)(2,1)S(1)} %get-tuple-element.14), channel_id=1, source_target_pairs={{0,2},{1,3},{2,0},{3,1},{4,6},{5,7},{6,4},{7,5},{8,10},{9,11},{10,... | collective-permute-start | bytes 393224 | tf_op jit(solution)/shard_map/ppermute | solution.py:23
  (35 other events, 294.3 us)

commit v2 on v0

v2 whole, which is shorter than its diff:
```python
import functools

import jax
import jax.numpy as jnp
from jax import lax
from jax.experimental import pallas as pl
from jax.experimental.pallas import tpu as pltpu
from jax.sharding import PartitionSpec as P

QUERY_HEADS = 64
KEY_VALUE_HEADS = 4
HEAD_SIZE = 128
SLOT_CAPACITY = 256

epsilon = 1e-05

F32, BF16 = jnp.float32, jnp.bfloat16
LANES = 128
FLOWS = 3

ATTN, FFN = 8, 16
SAME_CORE = [[2 * chip + core for chip in range(FFN // 2)] for core in range(2)]


def over_core(value):
    pairs = [(n, n ^ 1) for n in range(FFN)]
    return lax.ppermute(value, "ffn", pairs)


def over_chips(blocks):
    return lax.all_to_all(blocks, "ffn", 0, 0, tiled=True, axis_index_groups=SAME_CORE)


AXES = ((2, 4, 1), (4, 1, 2))
ORDERS = ((0, 1, 2), (1, 2, 0), (2, 0, 1))


def gray(place):
    return place ^ ((place & 4) >> 1)


def over_cube(value, axis):
    pairs = []
    for a in range(ATTN):
        for f in range(FFN):
            to_a = gray(gray(a) ^ AXES[f & 1][axis])
            pairs.append((a * FFN + f, to_a * FFN + f))
    return lax.ppermute(value, ("attn", "ffn"), pairs)


def cube_sum(sent, kept, order):
    for axis in order:
        total = kept.astype(F32) + over_cube(sent, axis).astype(F32)
        middle = total.shape[0] // 2
        sent, kept = total[:middle].astype(BF16), total[middle:]
    return total[0]


def cube_gather(own, order):
    own = own[None]
    for axis in order[:0:-1]:
        own = jnp.concatenate([over_cube(own, axis), own])
    return over_cube(own, order[0]), own


VMEM = pl.BlockSpec(memory_space=pltpu.VMEM)
SMEM = pl.BlockSpec(memory_space=pltpu.SMEM)
HBM = pl.BlockSpec(memory_space=pl.ANY)
TILE = 256
VMEM_LIMIT = 24 * 2**20


def load_kernel(count, *refs):
    arrived = refs[-1]
    copies = [
        pltpu.make_async_copy(refs[n], refs[count + n], arrived.at[n]) for n in range(count)
    ]
    for copy in copies:
        copy.start()
    for copy in copies:
        copy.wait()


def load(*arrays):
    count = len(arrays)
    return pl.pallas_call(
        functools.partial(load_kernel, count),
        out_shape=[jax.ShapeDtypeStruct(array.shape, array.dtype) for array in arrays],
        in_specs=[HBM] * count,
        out_specs=[VMEM] * count,
        scratch_shapes=[pltpu.SemaphoreType.DMA((count,))],
        compiler_params=pltpu.CompilerParams(vmem_limit_bytes=VMEM_LIMIT),
        cost_estimate=pl.CostEstimate(
            flops=0,
            bytes_accessed=sum(2 * array.size * array.dtype.itemsize for array in arrays),
            transcendentals=0,
        ),
    )(*arrays)


def gate_up_kernel(cut, place, x, w_gate, w_up, sent, kept, placed):
    batch = sent.shape[1]

    def store(value, at):
        for block in range(ATTN):
            part = value[block * batch : (block + 1) * batch]
            placed[place[block], :, at : at + value.shape[1]] = part

    at = 0
    for weights in (w_gate, w_up):
        for start in range(cut.start, cut.stop, TILE):
            columns = slice(start, min(start + TILE, cut.stop))
            product = jnp.dot(x[...], weights[:, columns], preferred_element_type=F32)
            store(product.astype(BF16), at)
            at += columns.stop - columns.start
    sent[...] = placed[: ATTN // 2]
    kept[...] = placed[ATTN // 2 :]


def first_gate_up_kernel(cut, place, own, other, w_gate, w_up, sent, kept, x, placed):
    depth = x.shape[1]
    half = own.shape[0]
    x[:half] = own[:, :depth]
    x[half:] = other[:, :depth]
    batch = sent.shape[1]
    for block in range(ATTN):
        rows, row = (own, block * batch) if block < ATTN // 2 else (other, block * batch - half)
        placed[place[block], :, 2 * (cut.stop - cut.start) :] = rows[row : row + batch, depth:]
    gate_up_kernel(cut, place, x, w_gate, w_up, sent, kept, placed)


def gate_up(place, x, w_gate, w_up, cut):
    depth = w_gate.shape[0]
    rows = sum(part.shape[0] for part in x)
    width = 2 * (cut.stop - cut.start) + x[0].shape[1] - depth
    half = jax.ShapeDtypeStruct((ATTN // 2, rows // ATTN, width), BF16)
    whole = [jax.ShapeDtypeStruct((rows, depth), BF16)] * (len(x) - 1)
    body = first_gate_up_kernel if whole else gate_up_kernel
    return pl.pallas_call(
        functools.partial(body, cut),
        out_shape=[half, half] + whole,
        in_specs=[SMEM] + [VMEM] * (len(x) + 2),
        out_specs=[VMEM] * (2 + len(whole)),
        scratch_shapes=[pltpu.VMEM((ATTN, rows // ATTN, width), BF16)],
        compiler_params=pltpu.CompilerParams(vmem_limit_bytes=VMEM_LIMIT),
        cost_estimate=pl.CostEstimate(
            flops=2 * rows * depth * width,
            bytes_accessed=2 * depth * width + 2 * rows * depth,
            transcendentals=0,
        ),
    )(place, *x, w_gate, w_up)


def down_kernel(place, *refs):
    parts, (w_down, own, other, hidden) = refs[: 2 * FLOWS], refs[2 * FLOWS :]
    at = 0
    for flow in range(FLOWS):
        batch, width = parts[2 * flow].shape[1:]
        for block in range(ATTN):
            part = parts[2 * flow + block // (ATTN // 2)][block % (ATTN // 2)]
            row = pl.multiple_of(place[flow, block] * batch, batch)
            hidden[pl.ds(row, batch), at : at + width] = part
        at += width
    half = own.shape[0]
    for start in range(0, own.shape[1], TILE):
        columns = slice(start, start + TILE)
        product = jnp.dot(hidden[...], w_down[:, columns], preferred_element_type=F32)
        own[:, columns] = product[:half]
        other[:, columns] = product[half:].astype(BF16)


def down(place, parts, w_down):
    units, width = w_down.shape
    rows = ATTN * parts[0].shape[1]
    return pl.pallas_call(
        down_kernel,
        out_shape=(
            jax.ShapeDtypeStruct((rows // 2, width), F32),
            jax.ShapeDtypeStruct((rows // 2, width), BF16),
        ),
        in_specs=[SMEM] + [VMEM] * (2 * FLOWS) + [VMEM],
        out_specs=(VMEM, VMEM),
        scratch_shapes=[pltpu.VMEM((rows, units), BF16)],
        compiler_params=pltpu.CompilerParams(vmem_limit_bytes=VMEM_LIMIT),
        cost_estimate=pl.CostEstimate(
            flops=2 * rows * units * width,
            bytes_accessed=2 * units * width + 2 * rows * units + 3 * rows * width,
            transcendentals=0,
        ),
    )(place, *parts, w_down)


def copies(value):
    return lax.optimization_barrier(jnp.broadcast_to(value, (8,) + value.shape))


def attend_kernel(lengths, queries, keys, values, own_key, own_value, out, heads, held, arrived, done):
    slots = queries.shape[0]
    group = QUERY_HEADS // KEY_VALUE_HEADS
    features = out.shape[2]
    fetches = []
    for slot in range(slots):
        fetches.append(
            (
                pltpu.make_async_copy(keys.at[slot], held.at[0, slot], arrived.at[0, slot]),
                pltpu.make_async_copy(values.at[slot], held.at[1, slot], arrived.at[1, slot]),
            )
        )
    for pair in fetches:
        for fetch in pair:
            fetch.start()
    wide = queries[...].astype(F32)
    for slot in range(slots):
        for head in range(QUERY_HEADS):
            heads[slot, head : head + 1] = wide[
                slot : slot + 1, head * HEAD_SIZE : (head + 1) * HEAD_SIZE
            ]
    factor = HEAD_SIZE ** (-0.5)
    position = lax.broadcasted_iota(jnp.int32, (QUERY_HEADS, SLOT_CAPACITY), 1)
    for slot in range(slots):
        for fetch in fetches[slot]:
            fetch.wait()
        query = heads[slot]
        own_score, scores = [], []
        for kv in range(KEY_VALUE_HEADS):
            at = slice(kv * HEAD_SIZE, (kv + 1) * HEAD_SIZE)
            part = query[kv * group : (kv + 1) * group]
            scores.append(
                lax.dot_general(
                    part.astype(BF16),
                    held[0, slot, :, at],
                    (((1,), (1,)), ((), ())),
                    preferred_element_type=F32,
                )
            )
            key = own_key[slot : slot + 1, at].astype(F32)
            own_score.append(jnp.sum(part * key, axis=-1, keepdims=True) * factor)
        scores = jnp.where(position < lengths[slot], jnp.concatenate(scores) * factor, -jnp.inf)
        own_score = jnp.concatenate(own_score)
        highest = jnp.maximum(jnp.max(scores, axis=-1, keepdims=True), own_score)
        weights = jnp.exp(scores - highest)
        own_weight = jnp.exp(own_score - highest)
        weight_sum = jnp.sum(weights, axis=-1, keepdims=True) + own_weight
        own_low = own_weight.astype(BF16).astype(F32)
        for kv in range(KEY_VALUE_HEADS):
            at = slice(kv * HEAD_SIZE, (kv + 1) * HEAD_SIZE)
            own_heads = slice(kv * group, (kv + 1) * group)
            combined = jnp.dot(
                weights[own_heads].astype(BF16), held[1, slot, :, at], preferred_element_type=F32
            )
            value = own_value[slot : slot + 1, at].astype(F32)
            combined = (combined + own_low[own_heads] * value) / weight_sum[own_heads]
            for n in range(group):
                first = (kv * group + n) * HEAD_SIZE
                to = first % features
                done[first // features, slot : slot + 1, to : to + HEAD_SIZE] = combined[n : n + 1]
    whole = done[...].astype(BF16)
    for device in range(ATTN):
        out[device * FFN : (device + 1) * FFN] = whole


def attend(queries, slot_key_cache, slot_value_cache, fresh_token_key, fresh_token_value, lengths):
    slots, features = queries.shape[0], QUERY_HEADS * HEAD_SIZE // FFN
    return pl.pallas_call(
        attend_kernel,
        out_shape=jax.ShapeDtypeStruct((ATTN * FFN, slots, features), BF16),
        in_specs=[SMEM, VMEM, HBM, HBM, VMEM, VMEM],
        out_specs=VMEM,
        scratch_shapes=[
            pltpu.VMEM((slots, QUERY_HEADS, HEAD_SIZE), F32),
            pltpu.VMEM((2,) + slot_key_cache.shape, BF16),
            pltpu.SemaphoreType.DMA((2, slots)),
            pltpu.VMEM((FFN, slots, features), F32),
        ],
        compiler_params=pltpu.CompilerParams(vmem_limit_bytes=58 * 2**20),
        cost_estimate=pl.CostEstimate(
            flops=4 * queries.size * SLOT_CAPACITY,
            bytes_accessed=4 * slot_key_cache.size,
            transcendentals=slots * QUERY_HEADS * SLOT_CAPACITY,
        ),
    )(lengths, queries, slot_key_cache, slot_value_cache, fresh_token_key, fresh_token_value)


def local(
    queries,
    slot_key_cache,
    slot_value_cache,
    fresh_token_key,
    fresh_token_value,
    lengths,
    slot_of,
    residual,
    w_out,
    norm_gain,
    w_gate,
    w_up,
    w_down,
):
    f = lax.axis_index("ffn")
    core = f % 2
    slots = queries.shape[0]
    features, width = w_out.shape
    units = w_up.shape[1]
    rows = residual.shape[0]
    share, batch, half = rows // FFN, rows // ATTN, rows // 2
    width_total = width * ATTN

    parts = attend(
        queries, slot_key_cache, slot_value_cache, fresh_token_key, fresh_token_value, lengths
    )
    held = lax.all_to_all(parts, ("attn", "ffn"), 0, 0, tiled=True).reshape(rows, features)

    by_core = slot_of.reshape(FFN // 2, 2, share)
    swapped = jnp.where(core == 0, by_core, by_core[:, ::-1])
    wanted = swapped.transpose(1, 0, 2).reshape(rows)
    choice = (wanted[:, None] == jnp.arange(rows, dtype=jnp.int32)[None, :]).astype(BF16)
    ordered = jnp.dot(choice, held, preferred_element_type=F32).astype(BF16)
    kept = lax.dynamic_slice_in_dim(residual, f * share, share, 0).astype(F32)

    def sum_over_cores(own, other):
        total = own + over_core(other).astype(F32)
        return total.astype(BF16).reshape(FFN // 2, share, width)

    def sum_over_chips(blocks):
        return jnp.sum(over_chips(blocks).astype(F32), axis=0)

    other = jnp.dot(ordered[half:], w_out, preferred_element_type=F32).astype(BF16)
    blocks = sum_over_cores(jnp.dot(ordered[:half], w_out, preferred_element_type=F32), other)
    blocks, *weights = lax.optimization_barrier((blocks, w_gate, w_up, w_down))
    w_gate, w_up, w_down = load(*weights)
    state = kept + sum_over_chips(blocks)
    squares = jnp.sum(state * state, axis=-1, keepdims=True)
    scaled = jnp.concatenate(
        [state * norm_gain.astype(F32), jnp.broadcast_to(squares, (share, LANES))], axis=1
    )
    scaled = over_chips(copies(scaled.astype(BF16))).reshape(half, width + LANES)
    x = [scaled, over_core(scaled)]

    eight = jnp.arange(ATTN, dtype=jnp.int32)
    attn_at = gray(lax.axis_index("attn"))

    def masks(flow):
        return [jnp.where(core == 0, AXES[0][axis], AXES[1][axis]) for axis in ORDERS[flow]]

    def place_of(flow):
        flipped = attn_at ^ gray(eight)
        bits = [((flipped & mask) == 0).astype(jnp.int32) for mask in masks(flow)]
        return bits[0] * 4 + bits[1] * 2 + bits[2]

    def block_at(flow):
        flips = [(1 - ((eight >> (2 - n)) & 1)) * mask for n, mask in enumerate(masks(flow))]
        return gray(attn_at ^ flips[0] ^ flips[1] ^ flips[2])

    tiles = units // LANES
    edges = [tiles * flow // FLOWS * LANES for flow in range(FLOWS + 1)]
    sums = []
    for flow in range(FLOWS):
        sent, kept, *whole = gate_up(
            place_of(flow), x, w_gate, w_up, slice(edges[flow], edges[flow + 1])
        )
        x = whole or x
        sums.append(cube_sum(sent, kept, ORDERS[flow]))
    scale = lax.rsqrt(sums[0][:, -1:] / width_total + epsilon)
    hidden = []
    for flow, both in enumerate(sums):
        size = edges[flow + 1] - edges[flow]
        gate, up = both[:, :size] * scale, both[:, size : 2 * size] * scale
        hidden += cube_gather((jax.nn.silu(gate) * up).astype(BF16), ORDERS[flow])
    blocks = jnp.stack([block_at(flow) for flow in range(FLOWS)])
    products = down(blocks, hidden, w_down)
    return (state + sum_over_chips(sum_over_cores(*products))).astype(BF16)


def solution(mesh):
    in_specs = (
        P(("attn", "ffn"), None),
        P(("attn", "ffn"), None, None),
        P(("attn", "ffn"), None, None),
        P(("attn", "ffn"), None),
        P(("attn", "ffn"), None),
        P(("attn", "ffn")),
        P(),
        P(None, "attn"),
        P("ffn", "attn"),
        P("attn"),
        P("attn", "ffn"),
        P("attn", "ffn"),
        P("ffn", "attn"),
    )
    out_specs = P("ffn", "attn")
    return jax.shard_map(local, mesh=mesh, in_specs=in_specs, out_specs=out_specs, check_vma=False)
```

time: 649 us -> 187 us (0.29)
  waiting for transfers between devices: 517 us -> 77.1 us
  matrix products: 36.6 us -> 3.01 us
  Pallas kernels: 0 us -> 26.1 us
  starting transfers between devices: 7.42 us -> 30.2 us
  between operations: 13.2 us -> 0.43 us
  blocking collectives: 50.3 us -> 41.4 us
  local copies, waits for them, and re-layouts: 11.4 us -> 3.58 us
  other arithmetic: 11.8 us -> 4.63 us
    psum x2 -> x0, waiting for transfers between devices: 429 us -> none  [the longest x1 276 us: local(): gate_sum, up_sum = lax.psum((gate_part, up_part), 'attn')]
    reduce_scatter x1 -> x0, waiting for transfers between devices: 81.4 us -> none  [local(): lax.psum_scatter(jnp.dot(hidden, w_down, preferred_element_type=jnp.float...]
    ppermute x0 -> x21, waiting for transfers between devices: none -> 46.1 us  [the longest x18 40.8 us: over_cube(): return lax.ppermute(value, ('attn', 'ffn'), pairs)]
    all_to_all x0 -> x2, blocking collectives: none -> 41.4 us  [over_chips(): lax.all_to_all(blocks, 'ffn', 0, 0, tiled=True, axis_index_groups=SAME_CORE)]
    dot_general x7 -> x3, matrix products: 36.6 us -> 3.01 us  [the longest x1 1.78 us: local(): jnp.dot(ordered[:half], w_out, preferred_element_type=F32)]
    all_gather x1 -> x0, blocking collectives: 31.4 us -> none  [local(): lax.all_gather(exchanged, 'attn', axis=0, tiled=True)]
    pallas_call x0 -> x6, Pallas kernels: none -> 26.1 us  [the longest x3 11.1 us: gate_up(): pl.pallas_call(functools.partial(body, cut), out_shape=[half, half] + who...]
    all_to_all x1 -> x2, waiting for transfers between devices: 7.57 us -> 31.1 us  [the longest x1 17.7 us: over_chips(): lax.all_to_all(blocks, 'ffn', 0, 0, tiled=True, axis_index_groups=SAME_CORE)]
  transfers between devices with their start and end apart: 4 -> 23, of which waited for: 4 -> 16; matrix products, arithmetic and copies ran while one was open for 0% -> 1% of each run, Pallas kernels for 0% -> 5%
where the time goes in v2:
time: 187 us; the launch traced here: 186 us
  waiting for transfers between devices  77.1 us (41%)
  blocking collectives  41.4 us (22%)
  starting transfers between devices  30.2 us (16%)
  Pallas kernels  26.1 us (14%)
  other arithmetic  4.63 us (2%)
  local copies, waits for them, and re-layouts  3.58 us (2%)
  matrix products  3.01 us (2%)
    all_to_all x2, blocking collectives, over_chips(): lax.all_to_all(blocks, 'ffn', 0, 0, tiled=True, axis_index_groups=SAME_CORE)  41.4 us
    ppermute x18, waiting for transfers between devices, over_cube(): return lax.ppermute(value, ('attn', 'ffn'), pairs)  40.8 us
    all_to_all x1, waiting for transfers between devices, over_chips(): lax.all_to_all(blocks, 'ffn', 0, 0, tiled=True, axis_index_groups=SAME_CORE)  17.7 us
    ppermute x18, starting transfers between devices, over_cube(): return lax.ppermute(value, ('attn', 'ffn'), pairs)  15.2 us
    all_to_all x1, waiting for transfers between devices, local(): lax.all_to_all(parts, ('attn', 'ffn'), 0, 0, tiled=True)  13.3 us
    all_to_all x1, starting transfers between devices, local(): lax.all_to_all(parts, ('attn', 'ffn'), 0, 0, tiled=True)  11.1 us
    pallas_call x3, Pallas kernels, gate_up(): pl.pallas_call(functools.partial(body, cut), out_shape=[half, half] + who...  11.1 us
    pallas_call x1, Pallas kernels, load(): pl.pallas_call(functools.partial(load_kernel, count), out_shape=[jax.Shap...  5.35 us
  transfers between devices with their start and end apart: 23, of which 16 were waited for; matrix products, arithmetic and copies ran while one was open for 1% of the time, Pallas kernels for 5%

profile of v2, /device:TPU:0, one launch (start us, length us, event | category | flops | bytes accessed | tf_op | source)
XLA Modules:
  0.0 186.5 jit_solution(12395038079221284159)
XLA Ops:
  0.0 5.0 %shard_map.127 = bf16[128,4,512]{2,1,0:T(4,128)(2,1)} custom-call(s32[4]{0:T(128)} %lengths.1, bf16[4,8192]{1,0:T(4,128)(2,1)} %queries.1, bf16[4,256,512]{2,1,0:T(8,128)(2,1)} %keys.1, bf16[4,256,512]{2,1,0:T(8,128)(2,1)} %values.1, bf16[4,512]{1,0:T(4,128)(2,1)} %own_key.1, bf16[4,512]{1,0:T(4,128)(2,1)} %own_value.1), custom_call_target="tpu_custom_call" | custom-call | flops 33554432 | bytes 2097152 | tf_op jit(solution)/shard_map/pallas_call | solution.py:264
  5.0 11.1 %all-to-all-start = ((bf16[128,4,512]{2,1,0:T(4,128)(2,1)}), bf16[128,4,512]{2,1,0:T(4,128)(2,1)S(1)}, u32[]{:S(2)}, u32[]{:S(2)}) async-start(bf16[128,4,512]{2,1,0:T(4,128)(2,1)} %shard_map.127), calls=%async_computation | async-start | bytes 1048576 | tf_op jit(solution)/shard_map/all_to_all | solution.py:311
  16.4 13.3 %all-to-all-done = bf16[128,4,512]{2,1,0:T(4,128)(2,1)S(1)} async-done(((bf16[128,4,512]{2,1,0:T(4,128)(2,1)}), bf16[128,4,512]{2,1,0:T(4,128)(2,1)S(1)}, u32[]{:S(2)}, u32[]{:S(2)}) %all-to-all-start) | async-done | bytes 524320 | tf_op jit(solution)/shard_map/all_to_all | solution.py:311
  31.2 2.6 %collective-permute-done = bf16[256,2048]{1,0:T(8,128)(2,1)S(1)} collective-permute-done((bf16[256,2048]{1,0:T(8,128)(2,1)S(1)}, bf16[256,2048]{1,0:T(8,128)(2,1)S(1)}, u32[]{:S(2)}, u32[]{:S(2)}) %collective-permute-start) | collective-permute-done | bytes 1048608 | tf_op jit(solution)/shard_map/ppermute | solution.py:27
  35.7 3.7 %all-to-all-start.1 = ((bf16[8,32,2048]{2,1,0:T(8,128)(2,1)}), bf16[8,32,2048]{2,1,0:T(8,128)(2,1)S(1)}, u32[]{:S(2)}, u32[]{:S(2)}) async-start(bf16[8,32,2048]{2,1,0:T(8,128)(2,1)} %bitcast.1), calls=%async_computation.1 | async-start | bytes 2097152 | tf_op jit(solution)/shard_map/all_to_all | solution.py:31
  39.4 17.7 %all-to-all-done.1 = bf16[8,32,2048]{2,1,0:T(8,128)(2,1)S(1)} async-done(((bf16[8,32,2048]{2,1,0:T(8,128)(2,1)}), bf16[8,32,2048]{2,1,0:T(8,128)(2,1)S(1)}, u32[]{:S(2)}, u32[]{:S(2)}) %all-to-all-start.1) | async-done | bytes 1048608 | tf_op jit(solution)/shard_map/all_to_all | solution.py:31
  58.5 20.9 %all_to_all.20 = bf16[8,32,2176]{2,1,0:T(8,128)(2,1)} all-to-all(bf16[8,32,2176]{2,1,0:T(8,128)(2,1)S(1)} %broadcast_in_dim.21), channel_id=1, replica_groups={{0,2,4,6,8,10,12,14},{1,3,5,7,9,11,13,15},{16,18,20,22,24,26,28,30},{17..., dimensions={0} | all-to-all | bytes 2228224 | tf_op jit(solution)/shard_map/all_to_all | solution.py:31
  79.4 2.9 %copy-done.2 = bf16[2048,1664]{1,0:T(8,128)(2,1)S(1)} copy-done((bf16[2048,1664]{1,0:T(8,128)(2,1)S(1)}, bf16[2048,1664]{1,0:T(8,128)(2,1)}, u32[]{:S(2)}) %copy-start.2) | copy-done | bytes 6815768
  82.3 5.3 %shard_map.128 = (bf16[2048,1664]{1,0:T(8,128)(2,1)S(1)}, bf16[2048,1664]{1,0:T(8,128)(2,1)S(1)}, bf16[1664,2048]{1,0:T(8,128)(2,1)S(1)}) custom-call(bf16[2048,1664]{1,0:T(8,128)(2,1)S(1)} %copy-done.2, bf16[2048,1664]{1,0:T(8,128)(2,1)} %refs_1_, bf16[1664,2048]{1,0:T(8,128)(2,1)} %refs_2_), custom_call_target="tpu_custom_call" | custom-call | bytes 40894464 | tf_op jit(solution)/shard_map/pallas_call | solution.py:86
  87.7 4.0 %shard_map.129 = (bf16[4,64,1152]{2,1,0:T(8,128)(2,1)S(1)}, bf16[4,64,1152]{2,1,0:T(8,128)(2,1)S(1)}, bf16[512,2048]{1,0:T(8,128)(2,1)S(1)}) custom-call(s32[8]{0:T(128)S(1)} %convert_add_fusion.6.place, bf16[256,2176]{1,0:T(8,128)(2,1)} %bitcast.2.own, bf16[256,2176]{1,0:T(8,128)(2,1)} %collective-permute-done.1.other, ...), custom_call_target="tpu_custom_call" | custom-call | flops 2415919104 | bytes 6815744 | tf_op jit(solution)/shard_map/pallas_call | solution.py:139
  91.8 3.0 %shard_map.130 = (bf16[4,64,1024]{2,1,0:T(8,128)(2,1)S(1)}, bf16[4,64,1024]{2,1,0:T(8,128)(2,1)S(1)}) custom-call(s32[8]{0:T(128)S(1)} %get-tuple-element.42.place, bf16[512,2048]{1,0:T(8,128)(2,1)S(1)} %get-tuple-element.29.x, bf16[2048,1664]{1,0:T(8,128)(2,1)S(1)} %get-tuple-element.25.w_gate, bf16[2048,1664]{1,0:T(8,128)(2,1)S(1)} %get-tuple-element.26.w_up), custom_call_target="tpu_custom_call" | custom-call | flops 2147483648 | bytes 6291456 | tf_op jit(solution)/shard_map/pallas_call | solution.py:139
  95.8 4.1 %shard_map.131 = (bf16[4,64,1280]{2,1,0:T(8,128)(2,1)S(1)}, bf16[4,64,1280]{2,1,0:T(8,128)(2,1)S(1)}) custom-call(s32[8]{0:T(128)S(1)} %get-tuple-element.41.place, bf16[512,2048]{1,0:T(8,128)(2,1)S(1)} %get-tuple-element.29.x, bf16[2048,1664]{1,0:T(8,128)(2,1)S(1)} %get-tuple-element.25.w_gate, bf16[2048,1664]{1,0:T(8,128)(2,1)S(1)} %get-tuple-element.26.w_up), custom_call_target="tpu_custom_call" | custom-call | flops 2684354560 | bytes 7340032 | tf_op jit(solution)/shard_map/pallas_call | solution.py:139
  100.5 10.4 %collective-permute-done.8 = bf16[4,64,1024]{2,1,0:T(8,128)(2,1)S(1)} collective-permute-done((bf16[4,64,1024]{2,1,0:T(8,128)(2,1)S(1)}, bf16[4,64,1024]{2,1,0:T(8,128)(2,1)S(1)}, u32[]{:S(2)}, u32[]{:S(2)}) %collective-permute-start.8) | collective-permute-done | bytes 524320 | tf_op jit(solution)/shard_map/ppermute | solution.py:48
  112.8 7.2 %collective-permute-done.9 = bf16[2,64,1024]{2,1,0:T(8,128)(2,1)S(1)} collective-permute-done((bf16[2,64,1024]{2,1,0:T(8,128)(2,1)S(1)}, bf16[2,64,1024]{2,1,0:T(8,128)(2,1)S(1)}, u32[]{:S(2)}, u32[]{:S(2)}) %collective-permute-start.9) | collective-permute-done | bytes 262176 | tf_op jit(solution)/shard_map/ppermute | solution.py:48
  122.4 2.3 %collective-permute-start.4 = (bf16[1,64,1152]{2,1,0:T(8,128)(2,1)S(1)}, bf16[1,64,1152]{2,1,0:T(8,128)(2,1)S(1)}, u32[]{:S(2)}, u32[]{:S(2)}) collective-permute-start(bf16[1,64,1152]{2,1,0:T(8,128)(2,1)S(1)} %slice.182), channel_id=1, source_target_pairs={{0,16},{1,33},{2,18},{3,35},{4,20},{5,37},{6,22},{7,39},{8,24},{9,... | collective-permute-start | bytes 442376 | tf_op jit(solution)/shard_map/ppermute | solution.py:48
  125.7 2.1 %collective-permute-done.4 = bf16[1,64,1152]{2,1,0:T(8,128)(2,1)S(1)} collective-permute-done((bf16[1,64,1152]{2,1,0:T(8,128)(2,1)S(1)}, bf16[1,64,1152]{2,1,0:T(8,128)(2,1)S(1)}, u32[]{:S(2)}, u32[]{:S(2)}) %collective-permute-start.4) | collective-permute-done | bytes 147488 | tf_op jit(solution)/shard_map/ppermute | solution.py:48
  131.1 2.2 %collective-permute-done.5 = bf16[1,64,512]{2,1,0:T(8,128)(2,1)S(1)} collective-permute-done((bf16[1,64,512]{2,1,0:T(8,128)(2,1)S(1)}, bf16[1,64,512]{2,1,0:T(8,128)(2,1)S(1)}, u32[]{:S(2)}, u32[]{:S(2)}) %collective-permute-start.5) | collective-permute-done | bytes 65568 | tf_op jit(solution)/shard_map/ppermute | solution.py:48
  133.8 3.2 %collective-permute-done.16 = bf16[1,64,1280]{2,1,0:T(8,128)(2,1)S(1)} collective-permute-done((bf16[1,64,1280]{2,1,0:T(8,128)(2,1)S(1)}, bf16[1,64,1280]{2,1,0:T(8,128)(2,1)S(1)}, u32[]{:S(2)}, u32[]{:S(2)}) %collective-permute-start.16) | collective-permute-done | bytes 163872 | tf_op jit(solution)/shard_map/ppermute | solution.py:48
  138.9 4.9 %collective-permute-done.17 = bf16[1,64,640]{2,1,0:T(8,128)(2,1)S(1)} collective-permute-done((bf16[1,64,640]{2,1,0:T(8,128)(2,1)S(1)}, bf16[1,64,640]{2,1,0:T(8,128)(2,1)S(1)}, u32[]{:S(2)}, u32[]{:S(2)}) %collective-permute-start.17) | collective-permute-done | bytes 81952 | tf_op jit(solution)/shard_map/ppermute | solution.py:48
  146.8 2.5 %collective-permute-done.18 = bf16[2,64,640]{2,1,0:T(8,128)(2,1)S(1)} collective-permute-done((bf16[2,64,640]{2,1,0:T(8,128)(2,1)S(1)}, bf16[2,64,640]{2,1,0:T(8,128)(2,1)S(1)}, u32[]{:S(2)}, u32[]{:S(2)}) %collective-permute-start.18) | collective-permute-done | bytes 163872 | tf_op jit(solution)/shard_map/ppermute | solution.py:48
  153.8 2.7 %collective-permute-done.19.refs_4_ = bf16[4,64,640]{2,1,0:T(8,128)(2,1)S(1)} collective-permute-done((bf16[4,64,640]{2,1,0:T(8,128)(2,1)S(1)}, bf16[4,64,640]{2,1,0:T(8,128)(2,1)S(1)}, u32[]{:S(2)}, u32[]{:S(2)}) %collective-permute-start.19) | collective-permute-done | bytes 327712 | tf_op jit(solution)/shard_map/ppermute | solution.py:48
  156.5 4.6 %shard_map.132 = (f32[256,2048]{1,0:T(8,128)S(1)}, bf16[256,2048]{1,0:T(8,128)(2,1)S(1)}) custom-call(s32[3,8]{1,0:T(4,128)S(1)} %pad_add_fusion.place, bf16[4,64,512]{2,1,0:T(8,128)(2,1)S(1)} %collective-permute-done.7.refs_0_, bf16[4,64,512]{2,1,0:T(8,128)(2,1)S(1)} %pad_maximum_fusion.1.refs_1_, bf16[4,64,512]{2,1,0:T(8,128)(2,1)S(1)} %collective-permute-done.13.refs_2_, ...), custom_call_target="tpu_custom_call" | custom-call | flops 3489660928 | bytes 11665408 | tf_op jit(solution)/shard_map/pallas_call | solution.py:175
  161.2 2.6 %collective-permute-done.20 = bf16[256,2048]{1,0:T(8,128)(2,1)S(1)} collective-permute-done((bf16[256,2048]{1,0:T(8,128)(2,1)S(1)}, bf16[256,2048]{1,0:T(8,128)(2,1)S(1)}, u32[]{:S(2)}, u32[]{:S(2)}) %collective-permute-start.20) | collective-permute-done | bytes 1048608 | tf_op jit(solution)/shard_map/ppermute | solution.py:27
  164.1 20.6 %all_to_all.21 = bf16[8,32,2048]{2,1,0:T(8,128)(2,1)S(1)} all-to-all(bf16[8,32,2048]{2,1,0:T(8,128)(2,1)S(1)} %bitcast.20), channel_id=1, replica_groups={{0,2,4,6,8,10,12,14},{1,3,5,7,9,11,13,15},{16,18,20,22,24,26,28,30},{17..., dimensions={0} | all-to-all | bytes 2097152 | tf_op jit(solution)/shard_map/all_to_all | solution.py:31
  (87 shorter events, 26.9 us)
Async XLA Ops:
  0.0 30.4 %copy-start = (bf16[512,2048]{1,0:T(8,128)(2,1)S(1)}, bf16[512,2048]{1,0:T(8,128)(2,1)}, u32[]{:S(2)}) copy-start(bf16[512,2048]{1,0:T(8,128)(2,1)} %param.21) | copy-start | bytes 6291460
  5.0 24.7 %all-to-all-start = ((bf16[128,4,512]{2,1,0:T(4,128)(2,1)}), bf16[128,4,512]{2,1,0:T(4,128)(2,1)S(1)}, u32[]{:S(2)}, u32[]{:S(2)}) async-start(bf16[128,4,512]{2,1,0:T(4,128)(2,1)} %shard_map.127), calls=%async_computation | async-start | bytes 1048576 | tf_op jit(solution)/shard_map/all_to_all | solution.py:311
  31.1 2.7 %collective-permute-start = (bf16[256,2048]{1,0:T(8,128)(2,1)S(1)}, bf16[256,2048]{1,0:T(8,128)(2,1)S(1)}, u32[]{:S(2)}, u32[]{:S(2)}) collective-permute-start(bf16[256,2048]{1,0:T(8,128)(2,1)S(1)} %convolution_convert_fusion), channel_id=1, source_target_pairs={{0,1},{1,0},{2,3},{3,2},{4,5},{5,4},{6,7},{7,6},{8,9},{9,8},{10,11... | collective-permute-start | bytes 3145736 | tf_op jit(solution)/shard_map/ppermute | solution.py:27
  35.7 21.5 %all-to-all-start.1 = ((bf16[8,32,2048]{2,1,0:T(8,128)(2,1)}), bf16[8,32,2048]{2,1,0:T(8,128)(2,1)S(1)}, u32[]{:S(2)}, u32[]{:S(2)}) async-start(bf16[8,32,2048]{2,1,0:T(8,128)(2,1)} %bitcast.1), calls=%async_computation.1 | async-start | bytes 2097152 | tf_op jit(solution)/shard_map/all_to_all | solution.py:31
  79.4 8.3 %collective-permute-start.1 = (bf16[256,2176]{1,0:T(8,128)(2,1)}, bf16[256,2176]{1,0:T(8,128)(2,1)}, u32[]{:S(2)}, u32[]{:S(2)}) collective-permute-start(bf16[256,2176]{1,0:T(8,128)(2,1)} %bitcast.2.own), channel_id=1, source_target_pairs={{0,1},{1,0},{2,3},{3,2},{4,5},{5,4},{6,7},{7,6},{8,9},{9,8},{10,11... | collective-permute-start | bytes 3342344 | tf_op jit(solution)/shard_map/ppermute | solution.py:27
  94.8 16.1 %collective-permute-start.8 = (bf16[4,64,1024]{2,1,0:T(8,128)(2,1)S(1)}, bf16[4,64,1024]{2,1,0:T(8,128)(2,1)S(1)}, u32[]{:S(2)}, u32[]{:S(2)}) collective-permute-start(bf16[4,64,1024]{2,1,0:T(8,128)(2,1)S(1)} %get-tuple-element.31), channel_id=1, source_target_pairs={{0,96},{1,17},{2,98},{3,19},{4,100},{5,21},{6,102},{7,23},{8,104},... | collective-permute-start | bytes 1572872 | tf_op jit(solution)/shard_map/ppermute | solution.py:48
  95.8 15.4 %collective-permute-start.2 = (bf16[4,64,1152]{2,1,0:T(8,128)(2,1)S(1)}, bf16[4,64,1152]{2,1,0:T(8,128)(2,1)S(1)}, u32[]{:S(2)}, u32[]{:S(2)}) collective-permute-start(bf16[4,64,1152]{2,1,0:T(8,128)(2,1)S(1)} %get-tuple-element.28), channel_id=1, source_target_pairs={{0,32},{1,97},{2,34},{3,99},{4,36},{5,101},{6,38},{7,103},{8,40},{... | collective-permute-start | bytes 1769480 | tf_op jit(solution)/shard_map/ppermute | solution.py:48
  99.9 12.5 %collective-permute-start.14 = (bf16[4,64,1280]{2,1,0:T(8,128)(2,1)S(1)}, bf16[4,64,1280]{2,1,0:T(8,128)(2,1)S(1)}, u32[]{:S(2)}, u32[]{:S(2)}) collective-permute-start(bf16[4,64,1280]{2,1,0:T(8,128)(2,1)S(1)} %get-tuple-element.33), channel_id=1, source_target_pairs={{0,16},{1,33},{2,18},{3,35},{4,20},{5,37},{6,22},{7,39},{8,24},{9,... | collective-permute-start | bytes 1966088 | tf_op jit(solution)/shard_map/ppermute | solution.py:48
  111.1 9.0 %collective-permute-start.9 = (bf16[2,64,1024]{2,1,0:T(8,128)(2,1)S(1)}, bf16[2,64,1024]{2,1,0:T(8,128)(2,1)S(1)}, u32[]{:S(2)}, u32[]{:S(2)}) collective-permute-start(bf16[2,64,1024]{2,1,0:T(8,128)(2,1)S(1)} %slice.180), channel_id=1, source_target_pairs={{0,16},{1,33},{2,18},{3,35},{4,20},{5,37},{6,22},{7,39},{8,24},{9,... | collective-permute-start | bytes 786440 | tf_op jit(solution)/shard_map/ppermute | solution.py:48
  111.4 10.9 %collective-permute-start.3 = (bf16[2,64,1152]{2,1,0:T(8,128)(2,1)S(1)}, bf16[2,64,1152]{2,1,0:T(8,128)(2,1)S(1)}, u32[]{:S(2)}, u32[]{:S(2)}) collective-permute-start(bf16[2,64,1152]{2,1,0:T(8,128)(2,1)S(1)} %slice.179), channel_id=1, source_target_pairs={{0,96},{1,17},{2,98},{3,19},{4,100},{5,21},{6,102},{7,23},{8,104},... | collective-permute-start | bytes 884744 | tf_op jit(solution)/shard_map/ppermute | solution.py:48
  112.5 17.8 %collective-permute-start.15 = (bf16[2,64,1280]{2,1,0:T(8,128)(2,1)S(1)}, bf16[2,64,1280]{2,1,0:T(8,128)(2,1)S(1)}, u32[]{:S(2)}, u32[]{:S(2)}) collective-permute-start(bf16[2,64,1280]{2,1,0:T(8,128)(2,1)S(1)} %slice.178), channel_id=1, source_target_pairs={{0,32},{1,97},{2,34},{3,99},{4,36},{5,101},{6,38},{7,103},{8,40},{... | collective-permute-start | bytes 983048 | tf_op jit(solution)/shard_map/ppermute | solution.py:48
  120.1 5.5 %collective-permute-start.10 = (bf16[1,64,1024]{2,1,0:T(8,128)(2,1)S(1)}, bf16[1,64,1024]{2,1,0:T(8,128)(2,1)S(1)}, u32[]{:S(2)}, u32[]{:S(2)}) collective-permute-start(bf16[1,64,1024]{2,1,0:T(8,128)(2,1)S(1)} %slice.183), channel_id=1, source_target_pairs={{0,32},{1,97},{2,34},{3,99},{4,36},{5,101},{6,38},{7,103},{8,40},{... | collective-permute-start | bytes 393224 | tf_op jit(solution)/shard_map/ppermute | solution.py:48
  122.4 5.5 %collective-permute-start.4 = (bf16[1,64,1152]{2,1,0:T(8,128)(2,1)S(1)}, bf16[1,64,1152]{2,1,0:T(8,128)(2,1)S(1)}, u32[]{:S(2)}, u32[]{:S(2)}) collective-permute-start(bf16[1,64,1152]{2,1,0:T(8,128)(2,1)S(1)} %slice.182), channel_id=1, source_target_pairs={{0,16},{1,33},{2,18},{3,35},{4,20},{5,37},{6,22},{7,39},{8,24},{9,... | collective-permute-start | bytes 442376 | tf_op jit(solution)/shard_map/ppermute | solution.py:48
  128.2 5.0 %collective-permute-start.5 = (bf16[1,64,512]{2,1,0:T(8,128)(2,1)S(1)}, bf16[1,64,512]{2,1,0:T(8,128)(2,1)S(1)}, u32[]{:S(2)}, u32[]{:S(2)}) collective-permute-start(bf16[1,64,512]{2,1,0:T(8,128)(2,1)S(1)} %get-tuple-element.40), channel_id=1, source_target_pairs={{0,16},{1,33},{2,18},{3,35},{4,20},{5,37},{6,22},{7,39},{8,24},{9,... | collective-permute-start | bytes 196616 | tf_op jit(solution)/shard_map/ppermute | solution.py:48
  130.4 6.6 %collective-permute-start.16 = (bf16[1,64,1280]{2,1,0:T(8,128)(2,1)S(1)}, bf16[1,64,1280]{2,1,0:T(8,128)(2,1)S(1)}, u32[]{:S(2)}, u32[]{:S(2)}) collective-permute-start(bf16[1,64,1280]{2,1,0:T(8,128)(2,1)S(1)} %slice.181), channel_id=1, source_target_pairs={{0,96},{1,17},{2,98},{3,19},{4,100},{5,21},{6,102},{7,23},{8,104},... | collective-permute-start | bytes 491528 | tf_op jit(solution)/shard_map/ppermute | solution.py:48
  131.1 6.8 %collective-permute-start.11 = (bf16[1,64,512]{2,1,0:T(8,128)(2,1)S(1)}, bf16[1,64,512]{2,1,0:T(8,128)(2,1)S(1)}, u32[]{:S(2)}, u32[]{:S(2)}) collective-permute-start(bf16[1,64,512]{2,1,0:T(8,128)(2,1)S(1)} %get-tuple-element.39), channel_id=1, source_target_pairs={{0,32},{1,97},{2,34},{3,99},{4,36},{5,101},{6,38},{7,103},{8,40},{... | collective-permute-start | bytes 196616 | tf_op jit(solution)/shard_map/ppermute | solution.py:48
  133.3 10.7 %collective-permute-start.6 = (bf16[2,64,512]{2,1,0:T(8,128)(2,1)S(1)}, bf16[2,64,512]{2,1,0:T(8,128)(2,1)S(1)}, u32[]{:S(2)}, u32[]{:S(2)}) collective-permute-start(bf16[2,64,512]{2,1,0:T(8,128)(2,1)S(1)} %pad_maximum_fusion.5), channel_id=1, source_target_pairs={{0,96},{1,17},{2,98},{3,19},{4,100},{5,21},{6,102},{7,23},{8,104},... | collective-permute-start | bytes 393224 | tf_op jit(solution)/shard_map/ppermute | solution.py:48
  137.2 6.7 %collective-permute-start.17 = (bf16[1,64,640]{2,1,0:T(8,128)(2,1)S(1)}, bf16[1,64,640]{2,1,0:T(8,128)(2,1)S(1)}, u32[]{:S(2)}, u32[]{:S(2)}) collective-permute-start(bf16[1,64,640]{2,1,0:T(8,128)(2,1)S(1)} %fusion.15), channel_id=1, source_target_pairs={{0,96},{1,17},{2,98},{3,19},{4,100},{5,21},{6,102},{7,23},{8,104},... | collective-permute-start | bytes 245768 | tf_op jit(solution)/shard_map/ppermute | solution.py:48
  137.9 8.2 %collective-permute-start.12 = (bf16[2,64,512]{2,1,0:T(8,128)(2,1)S(1)}, bf16[2,64,512]{2,1,0:T(8,128)(2,1)S(1)}, u32[]{:S(2)}, u32[]{:S(2)}) collective-permute-start(bf16[2,64,512]{2,1,0:T(8,128)(2,1)S(1)} %pad_maximum_fusion.6), channel_id=1, source_target_pairs={{0,16},{1,33},{2,18},{3,35},{4,20},{5,37},{6,22},{7,39},{8,24},{9,... | collective-permute-start | bytes 393224 | tf_op jit(solution)/shard_map/ppermute | solution.py:48
  143.9 5.4 %collective-permute-start.18 = (bf16[2,64,640]{2,1,0:T(8,128)(2,1)S(1)}, bf16[2,64,640]{2,1,0:T(8,128)(2,1)S(1)}, u32[]{:S(2)}, u32[]{:S(2)}) collective-permute-start(bf16[2,64,640]{2,1,0:T(8,128)(2,1)S(1)} %pad_maximum_fusion.3), channel_id=1, source_target_pairs={{0,32},{1,97},{2,34},{3,99},{4,36},{5,101},{6,38},{7,103},{8,40},{... | collective-permute-start | bytes 491528 | tf_op jit(solution)/shard_map/ppermute | solution.py:48
  144.0 8.1 %collective-permute-start.7 = (bf16[4,64,512]{2,1,0:T(8,128)(2,1)S(1)}, bf16[4,64,512]{2,1,0:T(8,128)(2,1)S(1)}, u32[]{:S(2)}, u32[]{:S(2)}) collective-permute-start(bf16[4,64,512]{2,1,0:T(8,128)(2,1)S(1)} %pad_maximum_fusion.1.refs_1_), channel_id=1, source_target_pairs={{0,32},{1,97},{2,34},{3,99},{4,36},{5,101},{6,38},{7,103},{8,40},{... | collective-permute-start | bytes 786440 | tf_op jit(solution)/shard_map/ppermute | solution.py:48
  146.1 7.7 %collective-permute-start.13 = (bf16[4,64,512]{2,1,0:T(8,128)(2,1)S(1)}, bf16[4,64,512]{2,1,0:T(8,128)(2,1)S(1)}, u32[]{:S(2)}, u32[]{:S(2)}) collective-permute-start(bf16[4,64,512]{2,1,0:T(8,128)(2,1)S(1)} %pad_maximum_fusion.2.refs_3_), channel_id=1, source_target_pairs={{0,96},{1,17},{2,98},{3,19},{4,100},{5,21},{6,102},{7,23},{8,104},... | collective-permute-start | bytes 786440 | tf_op jit(solution)/shard_map/ppermute | solution.py:48
  149.3 7.2 %collective-permute-start.19 = (bf16[4,64,640]{2,1,0:T(8,128)(2,1)S(1)}, bf16[4,64,640]{2,1,0:T(8,128)(2,1)S(1)}, u32[]{:S(2)}, u32[]{:S(2)}) collective-permute-start(bf16[4,64,640]{2,1,0:T(8,128)(2,1)S(1)} %pad_maximum_fusion.refs_5_), channel_id=1, source_target_pairs={{0,16},{1,33},{2,18},{3,35},{4,20},{5,37},{6,22},{7,39},{8,24},{9,... | collective-permute-start | bytes 983048 | tf_op jit(solution)/shard_map/ppermute | solution.py:48
  161.1 2.7 %collective-permute-start.20 = (bf16[256,2048]{1,0:T(8,128)(2,1)S(1)}, bf16[256,2048]{1,0:T(8,128)(2,1)S(1)}, u32[]{:S(2)}, u32[]{:S(2)}) collective-permute-start(bf16[256,2048]{1,0:T(8,128)(2,1)S(1)} %get-tuple-element.36), channel_id=1, source_target_pairs={{0,1},{1,0},{2,3},{3,2},{4,5},{5,4},{6,7},{7,6},{8,9},{9,8},{10,11... | collective-permute-start | bytes 3145736 | tf_op jit(solution)/shard_map/ppermute | solution.py:27
  (4 other events, 45.2 us)

commit v3 on v2

--- a/solution.py
+++ b/solution.py
@@ -326,8 +326,8 @@
 
     other = jnp.dot(ordered[half:], w_out, preferred_element_type=F32).astype(BF16)
     blocks = sum_over_cores(jnp.dot(ordered[:half], w_out, preferred_element_type=F32), other)
-    blocks, *weights = lax.optimization_barrier((blocks, w_gate, w_up, w_down))
-    w_gate, w_up, w_down = load(*weights)
+    blocks, *weights = lax.optimization_barrier((blocks, w_gate, w_up))
+    w_gate, w_up = load(*weights)
     state = kept + sum_over_chips(blocks)
     squares = jnp.sum(state * state, axis=-1, keepdims=True)
     scaled = jnp.concatenate(
@@ -360,6 +360,8 @@
         )
         x = whole or x
         sums.append(cube_sum(sent, kept, ORDERS[flow]))
+    sums[0], w_down = lax.optimization_barrier((sums[0], w_down))
+    (w_down,) = load(w_down)
     scale = lax.rsqrt(sums[0][:, -1:] / width_total + epsilon)
     hidden = []
     for flow, both in enumerate(sums):

time: 187 us -> 184 us (0.984)
  Pallas kernels: 26.1 us -> 21.1 us
  local copies, waits for them, and re-layouts: 3.58 us -> 6.53 us
    pallas_call x1 -> x2, Pallas kernels: 5.35 us -> 1.39 us  [load(): pl.pallas_call(functools.partial(load_kernel, count), out_shape=[jax.Shap...]
    unnamed x10 -> x16, local copies, waits for them, and re-layouts: 2.95 us -> 5.89 us
  transfers between devices with their start and end apart: 23 -> 23, of which waited for: 16 -> 16; matrix products, arithmetic and copies ran while one was open for 1% -> 1% of each run, Pallas kernels for 5% -> 3%
where the time goes in v3:
time: 184 us
  waiting for transfers between devices  76.2 us (41%)
  blocking collectives  41.2 us (22%)
  starting transfers between devices  30.5 us (17%)
  Pallas kernels  21.1 us (11%)
  local copies, waits for them, and re-layouts  6.53 us (4%)
  other arithmetic  4.63 us (3%)
  matrix products  2.98 us (2%)
    all_to_all x2, blocking collectives, over_chips(): lax.all_to_all(blocks, 'ffn', 0, 0, tiled=True, axis_index_groups=SAME_CORE)  41.2 us
    ppermute x18, waiting for transfers between devices, over_cube(): return lax.ppermute(value, ('attn', 'ffn'), pairs)  39.9 us
    all_to_all x1, waiting for transfers between devices, over_chips(): lax.all_to_all(blocks, 'ffn', 0, 0, tiled=True, axis_index_groups=SAME_CORE)  17.7 us
    ppermute x18, starting transfers between devices, over_cube(): return lax.ppermute(value, ('attn', 'ffn'), pairs)  15.5 us
    all_to_all x1, waiting for transfers between devices, local(): lax.all_to_all(parts, ('attn', 'ffn'), 0, 0, tiled=True)  13.3 us
    all_to_all x1, starting transfers between devices, local(): lax.all_to_all(parts, ('attn', 'ffn'), 0, 0, tiled=True)  11.1 us
    pallas_call x3, Pallas kernels, gate_up(): pl.pallas_call(functools.partial(body, cut), out_shape=[half, half] + who...  10.1 us
    unnamed x16, local copies, waits for them, and re-layouts  5.89 us
  transfers between devices with their start and end apart: 23, of which 16 were waited for; matrix products, arithmetic and copies ran while one was open for 1% of the time, Pallas kernels for 3%

profile of v3, /device:TPU:0, one launch (start us, length us, event | category | flops | bytes accessed | tf_op | source)
XLA Modules:
  0.0 183.7 jit_solution(10294090838090772738)
XLA Ops:
  0.0 5.0 %shard_map.127 = bf16[128,4,512]{2,1,0:T(4,128)(2,1)} custom-call(s32[4]{0:T(128)} %lengths.1, bf16[4,8192]{1,0:T(4,128)(2,1)} %queries.1, bf16[4,256,512]{2,1,0:T(8,128)(2,1)} %keys.1, bf16[4,256,512]{2,1,0:T(8,128)(2,1)} %values.1, bf16[4,512]{1,0:T(4,128)(2,1)} %own_key.1, bf16[4,512]{1,0:T(4,128)(2,1)} %own_value.1), custom_call_target="tpu_custom_call" | custom-call | flops 33554432 | bytes 2097152 | tf_op jit(solution)/shard_map/pallas_call | solution.py:264
  5.0 11.1 %all-to-all-start = ((bf16[128,4,512]{2,1,0:T(4,128)(2,1)}), bf16[128,4,512]{2,1,0:T(4,128)(2,1)S(1)}, u32[]{:S(2)}, u32[]{:S(2)}) async-start(bf16[128,4,512]{2,1,0:T(4,128)(2,1)} %shard_map.127), calls=%async_computation | async-start | bytes 1048576 | tf_op jit(solution)/shard_map/all_to_all | solution.py:311
  16.4 13.3 %all-to-all-done = bf16[128,4,512]{2,1,0:T(4,128)(2,1)S(1)} async-done(((bf16[128,4,512]{2,1,0:T(4,128)(2,1)}), bf16[128,4,512]{2,1,0:T(4,128)(2,1)S(1)}, u32[]{:S(2)}, u32[]{:S(2)}) %all-to-all-start) | async-done | bytes 524320 | tf_op jit(solution)/shard_map/all_to_all | solution.py:311
  31.2 2.6 %collective-permute-done = bf16[256,2048]{1,0:T(8,128)(2,1)S(1)} collective-permute-done((bf16[256,2048]{1,0:T(8,128)(2,1)S(1)}, bf16[256,2048]{1,0:T(8,128)(2,1)S(1)}, u32[]{:S(2)}, u32[]{:S(2)}) %collective-permute-start) | collective-permute-done | bytes 1048608 | tf_op jit(solution)/shard_map/ppermute | solution.py:27
  35.6 3.7 %all-to-all-start.1 = ((bf16[8,32,2048]{2,1,0:T(8,128)(2,1)}), bf16[8,32,2048]{2,1,0:T(8,128)(2,1)S(1)}, u32[]{:S(2)}, u32[]{:S(2)}) async-start(bf16[8,32,2048]{2,1,0:T(8,128)(2,1)} %bitcast.1), calls=%async_computation.1 | async-start | bytes 2097152 | tf_op jit(solution)/shard_map/all_to_all | solution.py:31
  39.4 17.7 %all-to-all-done.1 = bf16[8,32,2048]{2,1,0:T(8,128)(2,1)S(1)} async-done(((bf16[8,32,2048]{2,1,0:T(8,128)(2,1)}), bf16[8,32,2048]{2,1,0:T(8,128)(2,1)S(1)}, u32[]{:S(2)}, u32[]{:S(2)}) %all-to-all-start.1) | async-done | bytes 1048608 | tf_op jit(solution)/shard_map/all_to_all | solution.py:31
  58.5 20.7 %all_to_all.20 = bf16[8,32,2176]{2,1,0:T(8,128)(2,1)S(1)} all-to-all(bf16[8,32,2176]{2,1,0:T(8,128)(2,1)S(1)} %broadcast_in_dim.21), channel_id=1, replica_groups={{0,2,4,6,8,10,12,14},{1,3,5,7,9,11,13,15},{16,18,20,22,24,26,28,30},{17..., dimensions={0} | all-to-all | bytes 2228224 | tf_op jit(solution)/shard_map/all_to_all | solution.py:31
  79.2 2.9 %copy-done.2 = bf16[2048,1664]{1,0:T(8,128)(2,1)S(1)} copy-done((bf16[2048,1664]{1,0:T(8,128)(2,1)S(1)}, bf16[2048,1664]{1,0:T(8,128)(2,1)}, u32[]{:S(2)}) %copy-start.2) | copy-done | bytes 6815768
  82.1 2.9 %copy-done.3 = bf16[2048,1664]{1,0:T(8,128)(2,1)S(1)} copy-done((bf16[2048,1664]{1,0:T(8,128)(2,1)S(1)}, bf16[2048,1664]{1,0:T(8,128)(2,1)}, u32[]{:S(2)}) %copy-start.3) | copy-done | bytes 6815768
  86.0 3.0 %shard_map.129 = (bf16[4,64,1152]{2,1,0:T(8,128)(2,1)S(1)}, bf16[4,64,1152]{2,1,0:T(8,128)(2,1)S(1)}, bf16[512,2048]{1,0:T(8,128)(2,1)S(1)}) custom-call(s32[8]{0:T(128)S(1)} %convert_add_fusion.6.place, bf16[256,2176]{1,0:T(8,128)(2,1)S(1)} %bitcast.23, bf16[256,2176]{1,0:T(8,128)(2,1)S(1)} %collective-permute-done.1.other, ...), custom_call_target="tpu_custom_call" | custom-call | flops 2415919104 | bytes 6815744 | tf_op jit(solution)/shard_map/pallas_call | solution.py:139
  89.0 3.0 %shard_map.130 = (bf16[4,64,1024]{2,1,0:T(8,128)(2,1)S(1)}, bf16[4,64,1024]{2,1,0:T(8,128)(2,1)S(1)}) custom-call(s32[8]{0:T(128)S(1)} %get-tuple-element.42.place, bf16[512,2048]{1,0:T(8,128)(2,1)S(1)} %get-tuple-element.29.x, bf16[2048,1664]{1,0:T(8,128)(2,1)S(1)} %get-tuple-element.24.w_gate, bf16[2048,1664]{1,0:T(8,128)(2,1)S(1)} %get-tuple-element.25.w_up), custom_call_target="tpu_custom_call" | custom-call | flops 2147483648 | bytes 6291456 | tf_op jit(solution)/shard_map/pallas_call | solution.py:139
  93.0 4.1 %shard_map.131 = (bf16[4,64,1280]{2,1,0:T(8,128)(2,1)S(1)}, bf16[4,64,1280]{2,1,0:T(8,128)(2,1)S(1)}) custom-call(s32[8]{0:T(128)S(1)} %get-tuple-element.41.place, bf16[512,2048]{1,0:T(8,128)(2,1)S(1)} %get-tuple-element.29.x, bf16[2048,1664]{1,0:T(8,128)(2,1)S(1)} %get-tuple-element.24.w_gate, bf16[2048,1664]{1,0:T(8,128)(2,1)S(1)} %get-tuple-element.25.w_up), custom_call_target="tpu_custom_call" | custom-call | flops 2684354560 | bytes 7340032 | tf_op jit(solution)/shard_map/pallas_call | solution.py:139
  97.8 10.3 %collective-permute-done.8 = bf16[4,64,1024]{2,1,0:T(8,128)(2,1)S(1)} collective-permute-done((bf16[4,64,1024]{2,1,0:T(8,128)(2,1)S(1)}, bf16[4,64,1024]{2,1,0:T(8,128)(2,1)S(1)}, u32[]{:S(2)}, u32[]{:S(2)}) %collective-permute-start.8) | collective-permute-done | bytes 524320 | tf_op jit(solution)/shard_map/ppermute | solution.py:48
  110.1 7.3 %collective-permute-done.9 = bf16[2,64,1024]{2,1,0:T(8,128)(2,1)S(1)} collective-permute-done((bf16[2,64,1024]{2,1,0:T(8,128)(2,1)S(1)}, bf16[2,64,1024]{2,1,0:T(8,128)(2,1)S(1)}, u32[]{:S(2)}, u32[]{:S(2)}) %collective-permute-start.9) | collective-permute-done | bytes 262176 | tf_op jit(solution)/shard_map/ppermute | solution.py:48
  119.6 2.4 %collective-permute-start.4 = (bf16[1,64,1152]{2,1,0:T(8,128)(2,1)S(1)}, bf16[1,64,1152]{2,1,0:T(8,128)(2,1)S(1)}, u32[]{:S(2)}, u32[]{:S(2)}) collective-permute-start(bf16[1,64,1152]{2,1,0:T(8,128)(2,1)S(1)} %slice.167), channel_id=1, source_target_pairs={{0,16},{1,33},{2,18},{3,35},{4,20},{5,37},{6,22},{7,39},{8,24},{9,... | collective-permute-start | bytes 442376 | tf_op jit(solution)/shard_map/ppermute | solution.py:48
  125.5 2.1 %collective-permute-start.5 = (bf16[1,64,512]{2,1,0:T(8,128)(2,1)S(1)}, bf16[1,64,512]{2,1,0:T(8,128)(2,1)S(1)}, u32[]{:S(2)}, u32[]{:S(2)}) collective-permute-start(bf16[1,64,512]{2,1,0:T(8,128)(2,1)S(1)} %get-tuple-element.40), channel_id=1, source_target_pairs={{0,16},{1,33},{2,18},{3,35},{4,20},{5,37},{6,22},{7,39},{8,24},{9,... | collective-permute-start | bytes 196616 | tf_op jit(solution)/shard_map/ppermute | solution.py:48
  128.4 2.1 %collective-permute-done.5 = bf16[1,64,512]{2,1,0:T(8,128)(2,1)S(1)} collective-permute-done((bf16[1,64,512]{2,1,0:T(8,128)(2,1)S(1)}, bf16[1,64,512]{2,1,0:T(8,128)(2,1)S(1)}, u32[]{:S(2)}, u32[]{:S(2)}) %collective-permute-start.5) | collective-permute-done | bytes 65568 | tf_op jit(solution)/shard_map/ppermute | solution.py:48
  131.1 3.1 %collective-permute-done.16 = bf16[1,64,1280]{2,1,0:T(8,128)(2,1)S(1)} collective-permute-done((bf16[1,64,1280]{2,1,0:T(8,128)(2,1)S(1)}, bf16[1,64,1280]{2,1,0:T(8,128)(2,1)S(1)}, u32[]{:S(2)}, u32[]{:S(2)}) %collective-permute-start.16) | collective-permute-done | bytes 163872 | tf_op jit(solution)/shard_map/ppermute | solution.py:48
  136.2 4.9 %collective-permute-done.17 = bf16[1,64,640]{2,1,0:T(8,128)(2,1)S(1)} collective-permute-done((bf16[1,64,640]{2,1,0:T(8,128)(2,1)S(1)}, bf16[1,64,640]{2,1,0:T(8,128)(2,1)S(1)}, u32[]{:S(2)}, u32[]{:S(2)}) %collective-permute-start.17) | collective-permute-done | bytes 81952 | tf_op jit(solution)/shard_map/ppermute | solution.py:48
  144.1 2.4 %collective-permute-done.18 = bf16[2,64,640]{2,1,0:T(8,128)(2,1)S(1)} collective-permute-done((bf16[2,64,640]{2,1,0:T(8,128)(2,1)S(1)}, bf16[2,64,640]{2,1,0:T(8,128)(2,1)S(1)}, u32[]{:S(2)}, u32[]{:S(2)}) %collective-permute-start.18) | collective-permute-done | bytes 163872 | tf_op jit(solution)/shard_map/ppermute | solution.py:48
  151.1 2.7 %collective-permute-done.19.refs_4_ = bf16[4,64,640]{2,1,0:T(8,128)(2,1)S(1)} collective-permute-done((bf16[4,64,640]{2,1,0:T(8,128)(2,1)S(1)}, bf16[4,64,640]{2,1,0:T(8,128)(2,1)S(1)}, u32[]{:S(2)}, u32[]{:S(2)}) %collective-permute-start.19) | collective-permute-done | bytes 327712 | tf_op jit(solution)/shard_map/ppermute | solution.py:48
  153.7 4.6 %shard_map.133 = (f32[256,2048]{1,0:T(8,128)S(1)}, bf16[256,2048]{1,0:T(8,128)(2,1)S(1)}) custom-call(s32[3,8]{1,0:T(4,128)S(1)} %pad_add_fusion.place, bf16[4,64,512]{2,1,0:T(8,128)(2,1)S(1)} %collective-permute-done.7.refs_0_, bf16[4,64,512]{2,1,0:T(8,128)(2,1)S(1)} %pad_maximum_fusion.1.refs_1_, bf16[4,64,512]{2,1,0:T(8,128)(2,1)S(1)} %collective-permute-done.13.refs_2_, ...), custom_call_target="tpu_custom_call" | custom-call | flops 3489660928 | bytes 11665408 | tf_op jit(solution)/shard_map/pallas_call | solution.py:175
  158.4 2.6 %collective-permute-done.20 = bf16[256,2048]{1,0:T(8,128)(2,1)S(1)} collective-permute-done((bf16[256,2048]{1,0:T(8,128)(2,1)S(1)}, bf16[256,2048]{1,0:T(8,128)(2,1)S(1)}, u32[]{:S(2)}, u32[]{:S(2)}) %collective-permute-start.20) | collective-permute-done | bytes 1048608 | tf_op jit(solution)/shard_map/ppermute | solution.py:27
  161.4 20.5 %all_to_all.21 = bf16[8,32,2048]{2,1,0:T(8,128)(2,1)S(1)} all-to-all(bf16[8,32,2048]{2,1,0:T(8,128)(2,1)S(1)} %bitcast.24), channel_id=1, replica_groups={{0,2,4,6,8,10,12,14},{1,3,5,7,9,11,13,15},{16,18,20,22,24,26,28,30},{17..., dimensions={0} | all-to-all | bytes 2097152 | tf_op jit(solution)/shard_map/all_to_all | solution.py:31
  (95 shorter events, 28.0 us)
Async XLA Ops:
  5.0 24.7 %all-to-all-start = ((bf16[128,4,512]{2,1,0:T(4,128)(2,1)}), bf16[128,4,512]{2,1,0:T(4,128)(2,1)S(1)}, u32[]{:S(2)}, u32[]{:S(2)}) async-start(bf16[128,4,512]{2,1,0:T(4,128)(2,1)} %shard_map.127), calls=%async_computation | async-start | bytes 1048576 | tf_op jit(solution)/shard_map/all_to_all | solution.py:311
  31.1 2.7 %collective-permute-start = (bf16[256,2048]{1,0:T(8,128)(2,1)S(1)}, bf16[256,2048]{1,0:T(8,128)(2,1)S(1)}, u32[]{:S(2)}, u32[]{:S(2)}) collective-permute-start(bf16[256,2048]{1,0:T(8,128)(2,1)S(1)} %convolution_convert_fusion), channel_id=1, source_target_pairs={{0,1},{1,0},{2,3},{3,2},{4,5},{5,4},{6,7},{7,6},{8,9},{9,8},{10,11... | collective-permute-start | bytes 3145736 | tf_op jit(solution)/shard_map/ppermute | solution.py:27
  35.6 21.5 %all-to-all-start.1 = ((bf16[8,32,2048]{2,1,0:T(8,128)(2,1)}), bf16[8,32,2048]{2,1,0:T(8,128)(2,1)S(1)}, u32[]{:S(2)}, u32[]{:S(2)}) async-start(bf16[8,32,2048]{2,1,0:T(8,128)(2,1)} %bitcast.1), calls=%async_computation.1 | async-start | bytes 2097152 | tf_op jit(solution)/shard_map/all_to_all | solution.py:31
  79.2 6.8 %collective-permute-start.1 = (bf16[256,2176]{1,0:T(8,128)(2,1)S(1)}, bf16[256,2176]{1,0:T(8,128)(2,1)S(1)}, u32[]{:S(2)}, u32[]{:S(2)}) collective-permute-start(bf16[256,2176]{1,0:T(8,128)(2,1)S(1)} %bitcast.22), channel_id=1, source_target_pairs={{0,1},{1,0},{2,3},{3,2},{4,5},{5,4},{6,7},{7,6},{8,9},{9,8},{10,11... | collective-permute-start | bytes 3342344 | tf_op jit(solution)/shard_map/ppermute | solution.py:27
  92.0 16.1 %collective-permute-start.8 = (bf16[4,64,1024]{2,1,0:T(8,128)(2,1)S(1)}, bf16[4,64,1024]{2,1,0:T(8,128)(2,1)S(1)}, u32[]{:S(2)}, u32[]{:S(2)}) collective-permute-start(bf16[4,64,1024]{2,1,0:T(8,128)(2,1)S(1)} %get-tuple-element.31), channel_id=1, source_target_pairs={{0,96},{1,17},{2,98},{3,19},{4,100},{5,21},{6,102},{7,23},{8,104},... | collective-permute-start | bytes 1572872 | tf_op jit(solution)/shard_map/ppermute | solution.py:48
  93.0 15.4 %collective-permute-start.2 = (bf16[4,64,1152]{2,1,0:T(8,128)(2,1)S(1)}, bf16[4,64,1152]{2,1,0:T(8,128)(2,1)S(1)}, u32[]{:S(2)}, u32[]{:S(2)}) collective-permute-start(bf16[4,64,1152]{2,1,0:T(8,128)(2,1)S(1)} %get-tuple-element.27), channel_id=1, source_target_pairs={{0,32},{1,97},{2,34},{3,99},{4,36},{5,101},{6,38},{7,103},{8,40},{... | collective-permute-start | bytes 1769480 | tf_op jit(solution)/shard_map/ppermute | solution.py:48
  97.1 12.5 %collective-permute-start.14 = (bf16[4,64,1280]{2,1,0:T(8,128)(2,1)S(1)}, bf16[4,64,1280]{2,1,0:T(8,128)(2,1)S(1)}, u32[]{:S(2)}, u32[]{:S(2)}) collective-permute-start(bf16[4,64,1280]{2,1,0:T(8,128)(2,1)S(1)} %get-tuple-element.33), channel_id=1, source_target_pairs={{0,16},{1,33},{2,18},{3,35},{4,20},{5,37},{6,22},{7,39},{8,24},{9,... | collective-permute-start | bytes 1966088 | tf_op jit(solution)/shard_map/ppermute | solution.py:48
  108.3 9.0 %collective-permute-start.9 = (bf16[2,64,1024]{2,1,0:T(8,128)(2,1)S(1)}, bf16[2,64,1024]{2,1,0:T(8,128)(2,1)S(1)}, u32[]{:S(2)}, u32[]{:S(2)}) collective-permute-start(bf16[2,64,1024]{2,1,0:T(8,128)(2,1)S(1)} %slice.165), channel_id=1, source_target_pairs={{0,16},{1,33},{2,18},{3,35},{4,20},{5,37},{6,22},{7,39},{8,24},{9,... | collective-permute-start | bytes 786440 | tf_op jit(solution)/shard_map/ppermute | solution.py:48
  108.6 10.8 %collective-permute-start.3 = (bf16[2,64,1152]{2,1,0:T(8,128)(2,1)S(1)}, bf16[2,64,1152]{2,1,0:T(8,128)(2,1)S(1)}, u32[]{:S(2)}, u32[]{:S(2)}) collective-permute-start(bf16[2,64,1152]{2,1,0:T(8,128)(2,1)S(1)} %slice.164), channel_id=1, source_target_pairs={{0,96},{1,17},{2,98},{3,19},{4,100},{5,21},{6,102},{7,23},{8,104},... | collective-permute-start | bytes 884744 | tf_op jit(solution)/shard_map/ppermute | solution.py:48
  109.6 38.7 %slice-start = ((s8[6815744]{0:T(1024)(128)(4,1)}), s8[4194304]{0:T(1024)(128)(4,1)S(1)}, s32[]{:S(2)}) async-start(s8[6815744]{0:T(1024)(128)(4,1)} %bitcast.20), calls=%async_computation.4 | async-start | bytes 8388608
  109.8 17.8 %collective-permute-start.15 = (bf16[2,64,1280]{2,1,0:T(8,128)(2,1)S(1)}, bf16[2,64,1280]{2,1,0:T(8,128)(2,1)S(1)}, u32[]{:S(2)}, u32[]{:S(2)}) collective-permute-start(bf16[2,64,1280]{2,1,0:T(8,128)(2,1)S(1)} %slice.163), channel_id=1, source_target_pairs={{0,32},{1,97},{2,34},{3,99},{4,36},{5,101},{6,38},{7,103},{8,40},{... | collective-permute-start | bytes 983048 | tf_op jit(solution)/shard_map/ppermute | solution.py:48
  117.4 5.6 %collective-permute-start.10 = (bf16[1,64,1024]{2,1,0:T(8,128)(2,1)S(1)}, bf16[1,64,1024]{2,1,0:T(8,128)(2,1)S(1)}, u32[]{:S(2)}, u32[]{:S(2)}) collective-permute-start(bf16[1,64,1024]{2,1,0:T(8,128)(2,1)S(1)} %slice.168), channel_id=1, source_target_pairs={{0,32},{1,97},{2,34},{3,99},{4,36},{5,101},{6,38},{7,103},{8,40},{... | collective-permute-start | bytes 393224 | tf_op jit(solution)/shard_map/ppermute | solution.py:48
  119.6 5.5 %collective-permute-start.4 = (bf16[1,64,1152]{2,1,0:T(8,128)(2,1)S(1)}, bf16[1,64,1152]{2,1,0:T(8,128)(2,1)S(1)}, u32[]{:S(2)}, u32[]{:S(2)}) collective-permute-start(bf16[1,64,1152]{2,1,0:T(8,128)(2,1)S(1)} %slice.167), channel_id=1, source_target_pairs={{0,16},{1,33},{2,18},{3,35},{4,20},{5,37},{6,22},{7,39},{8,24},{9,... | collective-permute-start | bytes 442376 | tf_op jit(solution)/shard_map/ppermute | solution.py:48
  125.5 5.0 %collective-permute-start.5 = (bf16[1,64,512]{2,1,0:T(8,128)(2,1)S(1)}, bf16[1,64,512]{2,1,0:T(8,128)(2,1)S(1)}, u32[]{:S(2)}, u32[]{:S(2)}) collective-permute-start(bf16[1,64,512]{2,1,0:T(8,128)(2,1)S(1)} %get-tuple-element.40), channel_id=1, source_target_pairs={{0,16},{1,33},{2,18},{3,35},{4,20},{5,37},{6,22},{7,39},{8,24},{9,... | collective-permute-start | bytes 196616 | tf_op jit(solution)/shard_map/ppermute | solution.py:48
  127.7 6.6 %collective-permute-start.16 = (bf16[1,64,1280]{2,1,0:T(8,128)(2,1)S(1)}, bf16[1,64,1280]{2,1,0:T(8,128)(2,1)S(1)}, u32[]{:S(2)}, u32[]{:S(2)}) collective-permute-start(bf16[1,64,1280]{2,1,0:T(8,128)(2,1)S(1)} %slice.166), channel_id=1, source_target_pairs={{0,96},{1,17},{2,98},{3,19},{4,100},{5,21},{6,102},{7,23},{8,104},... | collective-permute-start | bytes 491528 | tf_op jit(solution)/shard_map/ppermute | solution.py:48
  128.4 6.8 %collective-permute-start.11 = (bf16[1,64,512]{2,1,0:T(8,128)(2,1)S(1)}, bf16[1,64,512]{2,1,0:T(8,128)(2,1)S(1)}, u32[]{:S(2)}, u32[]{:S(2)}) collective-permute-start(bf16[1,64,512]{2,1,0:T(8,128)(2,1)S(1)} %get-tuple-element.39), channel_id=1, source_target_pairs={{0,32},{1,97},{2,34},{3,99},{4,36},{5,101},{6,38},{7,103},{8,40},{... | collective-permute-start | bytes 196616 | tf_op jit(solution)/shard_map/ppermute | solution.py:48
  130.5 10.7 %collective-permute-start.6 = (bf16[2,64,512]{2,1,0:T(8,128)(2,1)S(1)}, bf16[2,64,512]{2,1,0:T(8,128)(2,1)S(1)}, u32[]{:S(2)}, u32[]{:S(2)}) collective-permute-start(bf16[2,64,512]{2,1,0:T(8,128)(2,1)S(1)} %pad_maximum_fusion.5), channel_id=1, source_target_pairs={{0,96},{1,17},{2,98},{3,19},{4,100},{5,21},{6,102},{7,23},{8,104},... | collective-permute-start | bytes 393224 | tf_op jit(solution)/shard_map/ppermute | solution.py:48
  134.4 6.7 %collective-permute-start.17 = (bf16[1,64,640]{2,1,0:T(8,128)(2,1)S(1)}, bf16[1,64,640]{2,1,0:T(8,128)(2,1)S(1)}, u32[]{:S(2)}, u32[]{:S(2)}) collective-permute-start(bf16[1,64,640]{2,1,0:T(8,128)(2,1)S(1)} %fusion.13), channel_id=1, source_target_pairs={{0,96},{1,17},{2,98},{3,19},{4,100},{5,21},{6,102},{7,23},{8,104},... | collective-permute-start | bytes 245768 | tf_op jit(solution)/shard_map/ppermute | solution.py:48
  135.2 8.2 %collective-permute-start.12 = (bf16[2,64,512]{2,1,0:T(8,128)(2,1)S(1)}, bf16[2,64,512]{2,1,0:T(8,128)(2,1)S(1)}, u32[]{:S(2)}, u32[]{:S(2)}) collective-permute-start(bf16[2,64,512]{2,1,0:T(8,128)(2,1)S(1)} %pad_maximum_fusion.6), channel_id=1, source_target_pairs={{0,16},{1,33},{2,18},{3,35},{4,20},{5,37},{6,22},{7,39},{8,24},{9,... | collective-permute-start | bytes 393224 | tf_op jit(solution)/shard_map/ppermute | solution.py:48
  141.1 5.4 %collective-permute-start.18 = (bf16[2,64,640]{2,1,0:T(8,128)(2,1)S(1)}, bf16[2,64,640]{2,1,0:T(8,128)(2,1)S(1)}, u32[]{:S(2)}, u32[]{:S(2)}) collective-permute-start(bf16[2,64,640]{2,1,0:T(8,128)(2,1)S(1)} %pad_maximum_fusion.3), channel_id=1, source_target_pairs={{0,32},{1,97},{2,34},{3,99},{4,36},{5,101},{6,38},{7,103},{8,40},{... | collective-permute-start | bytes 491528 | tf_op jit(solution)/shard_map/ppermute | solution.py:48
  141.3 8.1 %collective-permute-start.7 = (bf16[4,64,512]{2,1,0:T(8,128)(2,1)S(1)}, bf16[4,64,512]{2,1,0:T(8,128)(2,1)S(1)}, u32[]{:S(2)}, u32[]{:S(2)}) collective-permute-start(bf16[4,64,512]{2,1,0:T(8,128)(2,1)S(1)} %pad_maximum_fusion.1.refs_1_), channel_id=1, source_target_pairs={{0,32},{1,97},{2,34},{3,99},{4,36},{5,101},{6,38},{7,103},{8,40},{... | collective-permute-start | bytes 786440 | tf_op jit(solution)/shard_map/ppermute | solution.py:48
  143.4 7.7 %collective-permute-start.13 = (bf16[4,64,512]{2,1,0:T(8,128)(2,1)S(1)}, bf16[4,64,512]{2,1,0:T(8,128)(2,1)S(1)}, u32[]{:S(2)}, u32[]{:S(2)}) collective-permute-start(bf16[4,64,512]{2,1,0:T(8,128)(2,1)S(1)} %pad_maximum_fusion.2.refs_3_), channel_id=1, source_target_pairs={{0,96},{1,17},{2,98},{3,19},{4,100},{5,21},{6,102},{7,23},{8,104},... | collective-permute-start | bytes 786440 | tf_op jit(solution)/shard_map/ppermute | solution.py:48
  146.6 7.2 %collective-permute-start.19 = (bf16[4,64,640]{2,1,0:T(8,128)(2,1)S(1)}, bf16[4,64,640]{2,1,0:T(8,128)(2,1)S(1)}, u32[]{:S(2)}, u32[]{:S(2)}) collective-permute-start(bf16[4,64,640]{2,1,0:T(8,128)(2,1)S(1)} %pad_maximum_fusion.refs_5_), channel_id=1, source_target_pairs={{0,16},{1,33},{2,18},{3,35},{4,20},{5,37},{6,22},{7,39},{8,24},{9,... | collective-permute-start | bytes 983048 | tf_op jit(solution)/shard_map/ppermute | solution.py:48
  158.4 2.7 %collective-permute-start.20 = (bf16[256,2048]{1,0:T(8,128)(2,1)S(1)}, bf16[256,2048]{1,0:T(8,128)(2,1)S(1)}, u32[]{:S(2)}, u32[]{:S(2)}) collective-permute-start(bf16[256,2048]{1,0:T(8,128)(2,1)S(1)} %get-tuple-element.36), channel_id=1, source_target_pairs={{0,1},{1,0},{2,3},{3,2},{4,5},{5,4},{6,7},{7,6},{8,9},{9,8},{10,11... | collective-permute-start | bytes 3145736 | tf_op jit(solution)/shard_map/ppermute | solution.py:27
  (7 other events, 107.3 us)

commit v4 on v3

--- a/solution.py
+++ b/solution.py
@@ -326,9 +326,12 @@
 
     other = jnp.dot(ordered[half:], w_out, preferred_element_type=F32).astype(BF16)
     blocks = sum_over_cores(jnp.dot(ordered[:half], w_out, preferred_element_type=F32), other)
-    blocks, *weights = lax.optimization_barrier((blocks, w_gate, w_up))
-    w_gate, w_up = load(*weights)
-    state = kept + sum_over_chips(blocks)
+    blocks, w_up = lax.optimization_barrier((blocks, w_up))
+    (w_up,) = load(w_up)
+    blocks, w_up = lax.optimization_barrier((over_chips(blocks), w_up))
+    state = kept + jnp.sum(blocks.astype(F32), axis=0)
+    state, w_gate = lax.optimization_barrier((state, w_gate))
+    (w_gate,) = load(w_gate)
     squares = jnp.sum(state * state, axis=-1, keepdims=True)
     scaled = jnp.concatenate(
         [state * norm_gain.astype(F32), jnp.broadcast_to(squares, (share, LANES))], axis=1

time: 184 us -> 183 us (level)
  waiting for transfers between devices: 76.2 us -> 70.1 us
  local copies, waits for them, and re-layouts: 6.53 us -> 11 us
    all_to_all x1, waiting for transfers between devices: 17.7 us -> 11.5 us  [over_chips(): lax.all_to_all(blocks, 'ffn', 0, 0, tiled=True, axis_index_groups=SAME_CORE)]
    unnamed x16 -> x22, local copies, waits for them, and re-layouts: 5.89 us -> 10.4 us
where the time goes in v4:
time: 183 us; the launch traced here: 182 us
  waiting for transfers between devices  70.1 us (38%)
  blocking collectives  41.5 us (23%)
  starting transfers between devices  30.4 us (17%)
  Pallas kernels  22.2 us (12%)
  local copies, waits for them, and re-layouts  11 us (6%)
  other arithmetic  3.75 us (2%)
  matrix products  2.93 us (2%)
    all_to_all x2, blocking collectives, over_chips(): lax.all_to_all(blocks, 'ffn', 0, 0, tiled=True, axis_index_groups=SAME_CORE)  41.5 us
    ppermute x18, waiting for transfers between devices, over_cube(): return lax.ppermute(value, ('attn', 'ffn'), pairs)  40 us
    ppermute x18, starting transfers between devices, over_cube(): return lax.ppermute(value, ('attn', 'ffn'), pairs)  15.4 us
    all_to_all x1, waiting for transfers between devices, local(): lax.all_to_all(parts, ('attn', 'ffn'), 0, 0, tiled=True)  13.3 us
    all_to_all x1, waiting for transfers between devices, over_chips(): lax.all_to_all(blocks, 'ffn', 0, 0, tiled=True, axis_index_groups=SAME_CORE)  11.5 us
    all_to_all x1, starting transfers between devices, local(): lax.all_to_all(parts, ('attn', 'ffn'), 0, 0, tiled=True)  11.1 us
    pallas_call x3, Pallas kernels, gate_up(): pl.pallas_call(functools.partial(body, cut), out_shape=[half, half] + who...  11.1 us
    unnamed x22, local copies, waits for them, and re-layouts  10.4 us
  transfers between devices with their start and end apart: 23, of which 16 were waited for; matrix products, arithmetic and copies ran while one was open for 1% of the time, Pallas kernels for 3%

profile of v4, /device:TPU:0, one launch (start us, length us, event | category | flops | bytes accessed | tf_op | source)
XLA Modules:
  0.0 182.5 jit_solution(4328329305642806809)
XLA Ops:
  0.0 5.0 %shard_map.127 = bf16[128,4,512]{2,1,0:T(4,128)(2,1)} custom-call(s32[4]{0:T(128)} %lengths.1, bf16[4,8192]{1,0:T(4,128)(2,1)} %queries.1, bf16[4,256,512]{2,1,0:T(8,128)(2,1)} %keys.1, bf16[4,256,512]{2,1,0:T(8,128)(2,1)} %values.1, bf16[4,512]{1,0:T(4,128)(2,1)} %own_key.1, bf16[4,512]{1,0:T(4,128)(2,1)} %own_value.1), custom_call_target="tpu_custom_call" | custom-call | flops 33554432 | bytes 2097152 | tf_op jit(solution)/shard_map/pallas_call | solution.py:264
  5.0 11.1 %all-to-all-start = ((bf16[128,4,512]{2,1,0:T(4,128)(2,1)}), bf16[128,4,512]{2,1,0:T(4,128)(2,1)S(1)}, u32[]{:S(2)}, u32[]{:S(2)}) async-start(bf16[128,4,512]{2,1,0:T(4,128)(2,1)} %shard_map.127), calls=%async_computation | async-start | bytes 1048576 | tf_op jit(solution)/shard_map/all_to_all | solution.py:311
  16.4 13.3 %all-to-all-done = bf16[128,4,512]{2,1,0:T(4,128)(2,1)S(1)} async-done(((bf16[128,4,512]{2,1,0:T(4,128)(2,1)}), bf16[128,4,512]{2,1,0:T(4,128)(2,1)S(1)}, u32[]{:S(2)}, u32[]{:S(2)}) %all-to-all-start) | async-done | bytes 524320 | tf_op jit(solution)/shard_map/all_to_all | solution.py:311
  31.2 2.6 %collective-permute-done = bf16[256,2048]{1,0:T(8,128)(2,1)S(1)} collective-permute-done((bf16[256,2048]{1,0:T(8,128)(2,1)S(1)}, bf16[256,2048]{1,0:T(8,128)(2,1)S(1)}, u32[]{:S(2)}, u32[]{:S(2)}) %collective-permute-start) | collective-permute-done | bytes 1048608 | tf_op jit(solution)/shard_map/ppermute | solution.py:27
  35.6 3.7 %all-to-all-start.1 = ((bf16[8,32,2048]{2,1,0:T(8,128)(2,1)}), bf16[8,32,2048]{2,1,0:T(8,128)(2,1)S(1)}, u32[]{:S(2)}, u32[]{:S(2)}) async-start(bf16[8,32,2048]{2,1,0:T(8,128)(2,1)} %bitcast.1), calls=%async_computation.1 | async-start | bytes 2097152 | tf_op jit(solution)/shard_map/all_to_all | solution.py:31
  39.3 2.9 %copy-done.3 = bf16[2048,1664]{1,0:T(8,128)(2,1)S(1)} copy-done((bf16[2048,1664]{1,0:T(8,128)(2,1)S(1)}, bf16[2048,1664]{1,0:T(8,128)(2,1)}, u32[]{:S(2)}) %copy-start.3) | copy-done | bytes 6815768
  42.7 2.8 %copy-done.2 = bf16[2048,1664]{1,0:T(8,128)(2,1)} copy-done((bf16[2048,1664]{1,0:T(8,128)(2,1)}, bf16[2048,1664]{1,0:T(8,128)(2,1)S(1)}, u32[]{:S(2)}) %copy-start.2) | copy-done | bytes 6815768
  45.5 11.5 %all-to-all-done.1 = bf16[8,32,2048]{2,1,0:T(8,128)(2,1)S(1)} async-done(((bf16[8,32,2048]{2,1,0:T(8,128)(2,1)}), bf16[8,32,2048]{2,1,0:T(8,128)(2,1)S(1)}, u32[]{:S(2)}, u32[]{:S(2)}) %all-to-all-start.1) | async-done | bytes 1048608 | tf_op jit(solution)/shard_map/all_to_all | solution.py:31
  58.5 21.1 %all_to_all.20 = bf16[8,32,2176]{2,1,0:T(8,128)(2,1)} all-to-all(bf16[8,32,2176]{2,1,0:T(8,128)(2,1)S(1)} %broadcast_in_dim.21), channel_id=1, replica_groups={{0,2,4,6,8,10,12,14},{1,3,5,7,9,11,13,15},{16,18,20,22,24,26,28,30},{17..., dimensions={0} | all-to-all | bytes 2228224 | tf_op jit(solution)/shard_map/all_to_all | solution.py:31
  79.6 2.9 %copy-done.4 = bf16[2048,1664]{1,0:T(8,128)(2,1)S(1)} copy-done((bf16[2048,1664]{1,0:T(8,128)(2,1)S(1)}, bf16[2048,1664]{1,0:T(8,128)(2,1)}, u32[]{:S(2)}) %copy-start.4) | copy-done | bytes 6815768
  84.7 4.0 %shard_map.130 = (bf16[4,64,1152]{2,1,0:T(8,128)(2,1)S(1)}, bf16[4,64,1152]{2,1,0:T(8,128)(2,1)S(1)}, bf16[512,2048]{1,0:T(8,128)(2,1)S(1)}) custom-call(s32[8]{0:T(128)S(1)} %convert_add_fusion.6.place, bf16[256,2176]{1,0:T(8,128)(2,1)} %bitcast.2.own, bf16[256,2176]{1,0:T(8,128)(2,1)} %collective-permute-done.1.other, ...), custom_call_target="tpu_custom_call" | custom-call | flops 2415919104 | bytes 6815744 | tf_op jit(solution)/shard_map/pallas_call | solution.py:139
  88.8 3.0 %shard_map.131 = (bf16[4,64,1024]{2,1,0:T(8,128)(2,1)S(1)}, bf16[4,64,1024]{2,1,0:T(8,128)(2,1)S(1)}) custom-call(s32[8]{0:T(128)S(1)} %get-tuple-element.44.place, bf16[512,2048]{1,0:T(8,128)(2,1)S(1)} %get-tuple-element.31.x, bf16[2048,1664]{1,0:T(8,128)(2,1)S(1)} %shard_map.129.w_gate, bf16[2048,1664]{1,0:T(8,128)(2,1)S(1)} %bitcast.21), custom_call_target="tpu_custom_call" | custom-call | flops 2147483648 | bytes 6291456 | tf_op jit(solution)/shard_map/pallas_call | solution.py:139
  92.8 4.1 %shard_map.132 = (bf16[4,64,1280]{2,1,0:T(8,128)(2,1)S(1)}, bf16[4,64,1280]{2,1,0:T(8,128)(2,1)S(1)}) custom-call(s32[8]{0:T(128)S(1)} %get-tuple-element.43.place, bf16[512,2048]{1,0:T(8,128)(2,1)S(1)} %get-tuple-element.31.x, bf16[2048,1664]{1,0:T(8,128)(2,1)S(1)} %shard_map.129.w_gate, bf16[2048,1664]{1,0:T(8,128)(2,1)S(1)} %bitcast.21), custom_call_target="tpu_custom_call" | custom-call | flops 2684354560 | bytes 7340032 | tf_op jit(solution)/shard_map/pallas_call | solution.py:139
  97.5 10.3 %collective-permute-done.8 = bf16[4,64,1024]{2,1,0:T(8,128)(2,1)S(1)} collective-permute-done((bf16[4,64,1024]{2,1,0:T(8,128)(2,1)S(1)}, bf16[4,64,1024]{2,1,0:T(8,128)(2,1)S(1)}, u32[]{:S(2)}, u32[]{:S(2)}) %collective-permute-start.8) | collective-permute-done | bytes 524320 | tf_op jit(solution)/shard_map/ppermute | solution.py:48
  109.8 7.2 %collective-permute-done.9 = bf16[2,64,1024]{2,1,0:T(8,128)(2,1)S(1)} collective-permute-done((bf16[2,64,1024]{2,1,0:T(8,128)(2,1)S(1)}, bf16[2,64,1024]{2,1,0:T(8,128)(2,1)S(1)}, u32[]{:S(2)}, u32[]{:S(2)}) %collective-permute-start.9) | collective-permute-done | bytes 262176 | tf_op jit(solution)/shard_map/ppermute | solution.py:48
  119.3 2.4 %collective-permute-start.4 = (bf16[1,64,1152]{2,1,0:T(8,128)(2,1)S(1)}, bf16[1,64,1152]{2,1,0:T(8,128)(2,1)S(1)}, u32[]{:S(2)}, u32[]{:S(2)}) collective-permute-start(bf16[1,64,1152]{2,1,0:T(8,128)(2,1)S(1)} %slice.167), channel_id=1, source_target_pairs={{0,16},{1,33},{2,18},{3,35},{4,20},{5,37},{6,22},{7,39},{8,24},{9,... | collective-permute-start | bytes 442376 | tf_op jit(solution)/shard_map/ppermute | solution.py:48
  122.7 2.2 %collective-permute-done.4 = bf16[1,64,1152]{2,1,0:T(8,128)(2,1)S(1)} collective-permute-done((bf16[1,64,1152]{2,1,0:T(8,128)(2,1)S(1)}, bf16[1,64,1152]{2,1,0:T(8,128)(2,1)S(1)}, u32[]{:S(2)}, u32[]{:S(2)}) %collective-permute-start.4) | collective-permute-done | bytes 147488 | tf_op jit(solution)/shard_map/ppermute | solution.py:48
  130.9 3.1 %collective-permute-done.16 = bf16[1,64,1280]{2,1,0:T(8,128)(2,1)S(1)} collective-permute-done((bf16[1,64,1280]{2,1,0:T(8,128)(2,1)S(1)}, bf16[1,64,1280]{2,1,0:T(8,128)(2,1)S(1)}, u32[]{:S(2)}, u32[]{:S(2)}) %collective-permute-start.16) | collective-permute-done | bytes 163872 | tf_op jit(solution)/shard_map/ppermute | solution.py:48
  135.9 4.9 %collective-permute-done.17 = bf16[1,64,640]{2,1,0:T(8,128)(2,1)S(1)} collective-permute-done((bf16[1,64,640]{2,1,0:T(8,128)(2,1)S(1)}, bf16[1,64,640]{2,1,0:T(8,128)(2,1)S(1)}, u32[]{:S(2)}, u32[]{:S(2)}) %collective-permute-start.17) | collective-permute-done | bytes 81952 | tf_op jit(solution)/shard_map/ppermute | solution.py:48
  143.9 2.4 %collective-permute-done.18 = bf16[2,64,640]{2,1,0:T(8,128)(2,1)S(1)} collective-permute-done((bf16[2,64,640]{2,1,0:T(8,128)(2,1)S(1)}, bf16[2,64,640]{2,1,0:T(8,128)(2,1)S(1)}, u32[]{:S(2)}, u32[]{:S(2)}) %collective-permute-start.18) | collective-permute-done | bytes 163872 | tf_op jit(solution)/shard_map/ppermute | solution.py:48
  150.8 2.7 %collective-permute-done.19.refs_4_ = bf16[4,64,640]{2,1,0:T(8,128)(2,1)S(1)} collective-permute-done((bf16[4,64,640]{2,1,0:T(8,128)(2,1)S(1)}, bf16[4,64,640]{2,1,0:T(8,128)(2,1)S(1)}, u32[]{:S(2)}, u32[]{:S(2)}) %collective-permute-start.19) | collective-permute-done | bytes 327712 | tf_op jit(solution)/shard_map/ppermute | solution.py:48
  153.5 4.7 %shard_map.134 = (f32[256,2048]{1,0:T(8,128)S(1)}, bf16[256,2048]{1,0:T(8,128)(2,1)S(1)}) custom-call(s32[3,8]{1,0:T(4,128)S(1)} %pad_add_fusion.place, bf16[4,64,512]{2,1,0:T(8,128)(2,1)S(1)} %collective-permute-done.7.refs_0_, bf16[4,64,512]{2,1,0:T(8,128)(2,1)S(1)} %pad_maximum_fusion.1.refs_1_, bf16[4,64,512]{2,1,0:T(8,128)(2,1)S(1)} %collective-permute-done.13.refs_2_, ...), custom_call_target="tpu_custom_call" | custom-call | flops 3489660928 | bytes 11665408 | tf_op jit(solution)/shard_map/pallas_call | solution.py:175
  158.3 2.6 %collective-permute-done.20 = bf16[256,2048]{1,0:T(8,128)(2,1)S(1)} collective-permute-done((bf16[256,2048]{1,0:T(8,128)(2,1)S(1)}, bf16[256,2048]{1,0:T(8,128)(2,1)S(1)}, u32[]{:S(2)}, u32[]{:S(2)}) %collective-permute-start.20) | collective-permute-done | bytes 1048608 | tf_op jit(solution)/shard_map/ppermute | solution.py:27
  161.2 20.4 %all_to_all.21 = bf16[8,32,2048]{2,1,0:T(8,128)(2,1)S(1)} all-to-all(bf16[8,32,2048]{2,1,0:T(8,128)(2,1)S(1)} %bitcast.24), channel_id=1, replica_groups={{0,2,4,6,8,10,12,14},{1,3,5,7,9,11,13,15},{16,18,20,22,24,26,28,30},{17..., dimensions={0} | all-to-all | bytes 2097152 | tf_op jit(solution)/shard_map/all_to_all | solution.py:31
  (104 shorter events, 30.8 us)
Async XLA Ops:
  5.0 24.7 %all-to-all-start = ((bf16[128,4,512]{2,1,0:T(4,128)(2,1)}), bf16[128,4,512]{2,1,0:T(4,128)(2,1)S(1)}, u32[]{:S(2)}, u32[]{:S(2)}) async-start(bf16[128,4,512]{2,1,0:T(4,128)(2,1)} %shard_map.127), calls=%async_computation | async-start | bytes 1048576 | tf_op jit(solution)/shard_map/all_to_all | solution.py:311
  31.1 2.7 %collective-permute-start = (bf16[256,2048]{1,0:T(8,128)(2,1)S(1)}, bf16[256,2048]{1,0:T(8,128)(2,1)S(1)}, u32[]{:S(2)}, u32[]{:S(2)}) collective-permute-start(bf16[256,2048]{1,0:T(8,128)(2,1)S(1)} %convolution_convert_fusion), channel_id=1, source_target_pairs={{0,1},{1,0},{2,3},{3,2},{4,5},{5,4},{6,7},{7,6},{8,9},{9,8},{10,11... | collective-permute-start | bytes 3145736 | tf_op jit(solution)/shard_map/ppermute | solution.py:27
  35.6 21.5 %all-to-all-start.1 = ((bf16[8,32,2048]{2,1,0:T(8,128)(2,1)}), bf16[8,32,2048]{2,1,0:T(8,128)(2,1)S(1)}, u32[]{:S(2)}, u32[]{:S(2)}) async-start(bf16[8,32,2048]{2,1,0:T(8,128)(2,1)} %bitcast.1), calls=%async_computation.1 | async-start | bytes 2097152 | tf_op jit(solution)/shard_map/all_to_all | solution.py:31
  79.6 3.4 %collective-permute-start.1 = (bf16[256,2176]{1,0:T(8,128)(2,1)}, bf16[256,2176]{1,0:T(8,128)(2,1)}, u32[]{:S(2)}, u32[]{:S(2)}) collective-permute-start(bf16[256,2176]{1,0:T(8,128)(2,1)} %bitcast.2.own), channel_id=1, source_target_pairs={{0,1},{1,0},{2,3},{3,2},{4,5},{5,4},{6,7},{7,6},{8,9},{9,8},{10,11... | collective-permute-start | bytes 3342344 | tf_op jit(solution)/shard_map/ppermute | solution.py:27
  91.8 16.1 %collective-permute-start.8 = (bf16[4,64,1024]{2,1,0:T(8,128)(2,1)S(1)}, bf16[4,64,1024]{2,1,0:T(8,128)(2,1)S(1)}, u32[]{:S(2)}, u32[]{:S(2)}) collective-permute-start(bf16[4,64,1024]{2,1,0:T(8,128)(2,1)S(1)} %get-tuple-element.33), channel_id=1, source_target_pairs={{0,96},{1,17},{2,98},{3,19},{4,100},{5,21},{6,102},{7,23},{8,104},... | collective-permute-start | bytes 1572872 | tf_op jit(solution)/shard_map/ppermute | solution.py:48
  92.8 15.4 %collective-permute-start.2 = (bf16[4,64,1152]{2,1,0:T(8,128)(2,1)S(1)}, bf16[4,64,1152]{2,1,0:T(8,128)(2,1)S(1)}, u32[]{:S(2)}, u32[]{:S(2)}) collective-permute-start(bf16[4,64,1152]{2,1,0:T(8,128)(2,1)S(1)} %get-tuple-element.29), channel_id=1, source_target_pairs={{0,32},{1,97},{2,34},{3,99},{4,36},{5,101},{6,38},{7,103},{8,40},{... | collective-permute-start | bytes 1769480 | tf_op jit(solution)/shard_map/ppermute | solution.py:48
  96.9 12.5 %collective-permute-start.14 = (bf16[4,64,1280]{2,1,0:T(8,128)(2,1)S(1)}, bf16[4,64,1280]{2,1,0:T(8,128)(2,1)S(1)}, u32[]{:S(2)}, u32[]{:S(2)}) collective-permute-start(bf16[4,64,1280]{2,1,0:T(8,128)(2,1)S(1)} %get-tuple-element.35), channel_id=1, source_target_pairs={{0,16},{1,33},{2,18},{3,35},{4,20},{5,37},{6,22},{7,39},{8,24},{9,... | collective-permute-start | bytes 1966088 | tf_op jit(solution)/shard_map/ppermute | solution.py:48
  108.1 9.0 %collective-permute-start.9 = (bf16[2,64,1024]{2,1,0:T(8,128)(2,1)S(1)}, bf16[2,64,1024]{2,1,0:T(8,128)(2,1)S(1)}, u32[]{:S(2)}, u32[]{:S(2)}) collective-permute-start(bf16[2,64,1024]{2,1,0:T(8,128)(2,1)S(1)} %slice.165), channel_id=1, source_target_pairs={{0,16},{1,33},{2,18},{3,35},{4,20},{5,37},{6,22},{7,39},{8,24},{9,... | collective-permute-start | bytes 786440 | tf_op jit(solution)/shard_map/ppermute | solution.py:48
  108.4 10.8 %collective-permute-start.3 = (bf16[2,64,1152]{2,1,0:T(8,128)(2,1)S(1)}, bf16[2,64,1152]{2,1,0:T(8,128)(2,1)S(1)}, u32[]{:S(2)}, u32[]{:S(2)}) collective-permute-start(bf16[2,64,1152]{2,1,0:T(8,128)(2,1)S(1)} %slice.164), channel_id=1, source_target_pairs={{0,96},{1,17},{2,98},{3,19},{4,100},{5,21},{6,102},{7,23},{8,104},... | collective-permute-start | bytes 884744 | tf_op jit(solution)/shard_map/ppermute | solution.py:48
  109.3 38.7 %slice-start.2 = ((s8[6815744]{0:T(1024)(128)(4,1)}), s8[4194304]{0:T(1024)(128)(4,1)S(1)}, s32[]{:S(2)}) async-start(s8[6815744]{0:T(1024)(128)(4,1)} %bitcast.22), calls=%async_computation.6 | async-start | bytes 8388608
  109.5 17.8 %collective-permute-start.15 = (bf16[2,64,1280]{2,1,0:T(8,128)(2,1)S(1)}, bf16[2,64,1280]{2,1,0:T(8,128)(2,1)S(1)}, u32[]{:S(2)}, u32[]{:S(2)}) collective-permute-start(bf16[2,64,1280]{2,1,0:T(8,128)(2,1)S(1)} %slice.163), channel_id=1, source_target_pairs={{0,32},{1,97},{2,34},{3,99},{4,36},{5,101},{6,38},{7,103},{8,40},{... | collective-permute-start | bytes 983048 | tf_op jit(solution)/shard_map/ppermute | solution.py:48
  117.1 5.5 %collective-permute-start.10 = (bf16[1,64,1024]{2,1,0:T(8,128)(2,1)S(1)}, bf16[1,64,1024]{2,1,0:T(8,128)(2,1)S(1)}, u32[]{:S(2)}, u32[]{:S(2)}) collective-permute-start(bf16[1,64,1024]{2,1,0:T(8,128)(2,1)S(1)} %slice.168), channel_id=1, source_target_pairs={{0,32},{1,97},{2,34},{3,99},{4,36},{5,101},{6,38},{7,103},{8,40},{... | collective-permute-start | bytes 393224 | tf_op jit(solution)/shard_map/ppermute | solution.py:48
  119.3 5.5 %collective-permute-start.4 = (bf16[1,64,1152]{2,1,0:T(8,128)(2,1)S(1)}, bf16[1,64,1152]{2,1,0:T(8,128)(2,1)S(1)}, u32[]{:S(2)}, u32[]{:S(2)}) collective-permute-start(bf16[1,64,1152]{2,1,0:T(8,128)(2,1)S(1)} %slice.167), channel_id=1, source_target_pairs={{0,16},{1,33},{2,18},{3,35},{4,20},{5,37},{6,22},{7,39},{8,24},{9,... | collective-permute-start | bytes 442376 | tf_op jit(solution)/shard_map/ppermute | solution.py:48
  125.2 5.0 %collective-permute-start.5 = (bf16[1,64,512]{2,1,0:T(8,128)(2,1)S(1)}, bf16[1,64,512]{2,1,0:T(8,128)(2,1)S(1)}, u32[]{:S(2)}, u32[]{:S(2)}) collective-permute-start(bf16[1,64,512]{2,1,0:T(8,128)(2,1)S(1)} %get-tuple-element.42), channel_id=1, source_target_pairs={{0,16},{1,33},{2,18},{3,35},{4,20},{5,37},{6,22},{7,39},{8,24},{9,... | collective-permute-start | bytes 196616 | tf_op jit(solution)/shard_map/ppermute | solution.py:48
  127.4 6.6 %collective-permute-start.16 = (bf16[1,64,1280]{2,1,0:T(8,128)(2,1)S(1)}, bf16[1,64,1280]{2,1,0:T(8,128)(2,1)S(1)}, u32[]{:S(2)}, u32[]{:S(2)}) collective-permute-start(bf16[1,64,1280]{2,1,0:T(8,128)(2,1)S(1)} %slice.166), channel_id=1, source_target_pairs={{0,96},{1,17},{2,98},{3,19},{4,100},{5,21},{6,102},{7,23},{8,104},... | collective-permute-start | bytes 491528 | tf_op jit(solution)/shard_map/ppermute | solution.py:48
  128.1 6.8 %collective-permute-start.11 = (bf16[1,64,512]{2,1,0:T(8,128)(2,1)S(1)}, bf16[1,64,512]{2,1,0:T(8,128)(2,1)S(1)}, u32[]{:S(2)}, u32[]{:S(2)}) collective-permute-start(bf16[1,64,512]{2,1,0:T(8,128)(2,1)S(1)} %get-tuple-element.41), channel_id=1, source_target_pairs={{0,32},{1,97},{2,34},{3,99},{4,36},{5,101},{6,38},{7,103},{8,40},{... | collective-permute-start | bytes 196616 | tf_op jit(solution)/shard_map/ppermute | solution.py:48
  130.3 10.7 %collective-permute-start.6 = (bf16[2,64,512]{2,1,0:T(8,128)(2,1)S(1)}, bf16[2,64,512]{2,1,0:T(8,128)(2,1)S(1)}, u32[]{:S(2)}, u32[]{:S(2)}) collective-permute-start(bf16[2,64,512]{2,1,0:T(8,128)(2,1)S(1)} %pad_maximum_fusion.5), channel_id=1, source_target_pairs={{0,96},{1,17},{2,98},{3,19},{4,100},{5,21},{6,102},{7,23},{8,104},... | collective-permute-start | bytes 393224 | tf_op jit(solution)/shard_map/ppermute | solution.py:48
  134.2 6.7 %collective-permute-start.17 = (bf16[1,64,640]{2,1,0:T(8,128)(2,1)S(1)}, bf16[1,64,640]{2,1,0:T(8,128)(2,1)S(1)}, u32[]{:S(2)}, u32[]{:S(2)}) collective-permute-start(bf16[1,64,640]{2,1,0:T(8,128)(2,1)S(1)} %fusion.13), channel_id=1, source_target_pairs={{0,96},{1,17},{2,98},{3,19},{4,100},{5,21},{6,102},{7,23},{8,104},... | collective-permute-start | bytes 245768 | tf_op jit(solution)/shard_map/ppermute | solution.py:48
  134.9 8.2 %collective-permute-start.12 = (bf16[2,64,512]{2,1,0:T(8,128)(2,1)S(1)}, bf16[2,64,512]{2,1,0:T(8,128)(2,1)S(1)}, u32[]{:S(2)}, u32[]{:S(2)}) collective-permute-start(bf16[2,64,512]{2,1,0:T(8,128)(2,1)S(1)} %pad_maximum_fusion.6), channel_id=1, source_target_pairs={{0,16},{1,33},{2,18},{3,35},{4,20},{5,37},{6,22},{7,39},{8,24},{9,... | collective-permute-start | bytes 393224 | tf_op jit(solution)/shard_map/ppermute | solution.py:48
  140.9 5.4 %collective-permute-start.18 = (bf16[2,64,640]{2,1,0:T(8,128)(2,1)S(1)}, bf16[2,64,640]{2,1,0:T(8,128)(2,1)S(1)}, u32[]{:S(2)}, u32[]{:S(2)}) collective-permute-start(bf16[2,64,640]{2,1,0:T(8,128)(2,1)S(1)} %pad_maximum_fusion.3), channel_id=1, source_target_pairs={{0,32},{1,97},{2,34},{3,99},{4,36},{5,101},{6,38},{7,103},{8,40},{... | collective-permute-start | bytes 491528 | tf_op jit(solution)/shard_map/ppermute | solution.py:48
  141.0 8.1 %collective-permute-start.7 = (bf16[4,64,512]{2,1,0:T(8,128)(2,1)S(1)}, bf16[4,64,512]{2,1,0:T(8,128)(2,1)S(1)}, u32[]{:S(2)}, u32[]{:S(2)}) collective-permute-start(bf16[4,64,512]{2,1,0:T(8,128)(2,1)S(1)} %pad_maximum_fusion.1.refs_1_), channel_id=1, source_target_pairs={{0,32},{1,97},{2,34},{3,99},{4,36},{5,101},{6,38},{7,103},{8,40},{... | collective-permute-start | bytes 786440 | tf_op jit(solution)/shard_map/ppermute | solution.py:48
  143.1 7.7 %collective-permute-start.13 = (bf16[4,64,512]{2,1,0:T(8,128)(2,1)S(1)}, bf16[4,64,512]{2,1,0:T(8,128)(2,1)S(1)}, u32[]{:S(2)}, u32[]{:S(2)}) collective-permute-start(bf16[4,64,512]{2,1,0:T(8,128)(2,1)S(1)} %pad_maximum_fusion.2.refs_3_), channel_id=1, source_target_pairs={{0,96},{1,17},{2,98},{3,19},{4,100},{5,21},{6,102},{7,23},{8,104},... | collective-permute-start | bytes 786440 | tf_op jit(solution)/shard_map/ppermute | solution.py:48
  146.3 7.2 %collective-permute-start.19 = (bf16[4,64,640]{2,1,0:T(8,128)(2,1)S(1)}, bf16[4,64,640]{2,1,0:T(8,128)(2,1)S(1)}, u32[]{:S(2)}, u32[]{:S(2)}) collective-permute-start(bf16[4,64,640]{2,1,0:T(8,128)(2,1)S(1)} %pad_maximum_fusion.refs_5_), channel_id=1, source_target_pairs={{0,16},{1,33},{2,18},{3,35},{4,20},{5,37},{6,22},{7,39},{8,24},{9,... | collective-permute-start | bytes 983048 | tf_op jit(solution)/shard_map/ppermute | solution.py:48
  158.2 2.7 %collective-permute-start.20 = (bf16[256,2048]{1,0:T(8,128)(2,1)S(1)}, bf16[256,2048]{1,0:T(8,128)(2,1)S(1)}, u32[]{:S(2)}, u32[]{:S(2)}) collective-permute-start(bf16[256,2048]{1,0:T(8,128)(2,1)S(1)} %get-tuple-element.38), channel_id=1, source_target_pairs={{0,1},{1,0},{2,3},{3,2},{4,5},{5,4},{6,7},{7,6},{8,9},{9,8},{10,11... | collective-permute-start | bytes 3145736 | tf_op jit(solution)/shard_map/ppermute | solution.py:27
  (10 other events, 136.1 us)
